TPU v7x, 128 devices: a whole 4x4x4 slice. The times are simulated.
128 devices in a mesh: inp: 4 (over y_hi, core), wt: 4 (over x), out: 8 (over y_lo, z).
Axes of the slice: x: 4, y: 4 (y_hi: 2, y_lo: 2; y = y_hi * 2 + y_lo), z: 4, core: 2. Of those that a mesh axis runs over, the one named last changes fastest.
Arguments:
- tokens: bfloat16 [2, 4096, 2048], P(None, ('inp', 'wt'), 'out'), may hold values from -6 to 6
- gate_weight: bfloat16 [2048, 4096], P('out', ('wt', 'inp')), may hold values from -0.125 to 0.125
- up_weight: bfloat16 [2048, 4096], P('out', ('wt', 'inp')), may hold values from -0.125 to 0.125
- down_weight: bfloat16 [4096, 2048], P(('wt', 'inp'), 'out'), may hold values from -0.09375 to 0.09375
- cotangent: bfloat16 [2, 4096, 2048], P(None, ('inp', 'wt'), 'out'), may hold values from -3 to 3
Outputs:
- output: bfloat16 [2, 4096, 2048], P(None, ('inp', 'wt'), 'out')
- grad_tokens: bfloat16 [2, 4096, 2048], P(None, ('inp', 'wt'), 'out')
- grad_gate: float32 [2048, 4096], P('out', ('wt', 'inp'))
- grad_up: float32 [2048, 4096], P('out', ('wt', 'inp'))
- grad_down: float32 [4096, 2048], P(('wt', 'inp'), 'out')
All inputs are finite; a program needn't handle non-finite values.
Results may differ from a plain program's by a relative error of at most 0.035.
Values may be sent and summed in bfloat16 or wider, within the bound.
A program may use at most 128 MiB of HBM per device.

v0:
```python
import jax
import jax.numpy as jnp
from jax import lax
from jax.sharding import PartitionSpec as P


def activations(gate_sum, up_sum, back_sum):
    sigmoid_g = jax.nn.sigmoid(gate_sum)
    silu_g = gate_sum * sigmoid_g
    hidden = (silu_g * up_sum).astype(jnp.bfloat16)
    slope = sigmoid_g * (1.0 + gate_sum * (1.0 - sigmoid_g))
    grad_gate_act = (back_sum * up_sum * slope).astype(jnp.bfloat16)
    grad_up_act = (back_sum * silu_g).astype(jnp.bfloat16)
    return (hidden, grad_gate_act, grad_up_act)


def on_device(tokens, gate_weight, up_weight, down_weight, cotangent):
    in_block, cot_block = (
        lax.all_gather(tokens, "wt", axis=1, tiled=True),
        lax.all_gather(cotangent, "wt", axis=1, tiled=True),
    )
    gate_full, up_full = (
        lax.all_gather(gate_weight, "inp", axis=1, tiled=True),
        lax.all_gather(up_weight, "inp", axis=1, tiled=True),
    )
    down_full = lax.all_gather(down_weight, "inp", axis=0, tiled=True)
    gate_part = jnp.einsum("btd,df->btf", in_block, gate_full, preferred_element_type=jnp.float32)
    up_part = jnp.einsum("btd,df->btf", in_block, up_full, preferred_element_type=jnp.float32)
    back_part = jnp.einsum("btd,fd->btf", cot_block, down_full, preferred_element_type=jnp.float32)
    gate_sum, up_sum = (
        lax.psum_scatter(
            gate_part.astype(jnp.bfloat16), "out", scatter_dimension=1, tiled=True
        ).astype(jnp.float32),
        lax.psum_scatter(
            up_part.astype(jnp.bfloat16), "out", scatter_dimension=1, tiled=True
        ).astype(jnp.float32),
    )
    back_sum = lax.psum_scatter(
        back_part.astype(jnp.bfloat16), "out", scatter_dimension=1, tiled=True
    ).astype(jnp.float32)
    hidden_own, gate_act_own, up_act_own = activations(gate_sum, up_sum, back_sum)
    hidden_rows = lax.all_gather(hidden_own, "out", axis=1, tiled=True)
    grad_gate_rows, grad_up_rows = (
        lax.all_gather(gate_act_own, "out", axis=1, tiled=True),
        lax.all_gather(up_act_own, "out", axis=1, tiled=True),
    )
    output_part = jnp.einsum(
        "btf,fd->btd", hidden_rows, down_full, preferred_element_type=jnp.float32
    )
    output = lax.psum_scatter(
        output_part.astype(jnp.bfloat16), "wt", scatter_dimension=1, tiled=True
    )
    input_part = jnp.einsum(
        "btf,df->btd", grad_gate_rows, gate_full, preferred_element_type=jnp.float32
    )
    input_part = input_part + jnp.einsum(
        "btf,df->btd", grad_up_rows, up_full, preferred_element_type=jnp.float32
    )
    grad_tokens = lax.psum_scatter(
        input_part.astype(jnp.bfloat16), "wt", scatter_dimension=1, tiled=True
    )
    gate_term = jnp.einsum(
        "btd,btf->df", in_block, grad_gate_rows, preferred_element_type=jnp.float32
    )
    up_term = jnp.einsum("btd,btf->df", in_block, grad_up_rows, preferred_element_type=jnp.float32)
    grad_gate, grad_up = (
        lax.psum_scatter(
            gate_term.astype(jnp.bfloat16), "inp", scatter_dimension=1, tiled=True
        ).astype(jnp.float32),
        lax.psum_scatter(
            up_term.astype(jnp.bfloat16), "inp", scatter_dimension=1, tiled=True
        ).astype(jnp.float32),
    )
    down_term = jnp.einsum(
        "btf,btd->fd", hidden_rows, cot_block, preferred_element_type=jnp.float32
    )
    grad_down = lax.psum_scatter(
        down_term.astype(jnp.bfloat16), "inp", scatter_dimension=0, tiled=True
    ).astype(jnp.float32)
    return (output, grad_tokens, grad_gate, grad_up, grad_down)


def solution(mesh):
    in_specs = (
        P(None, ("inp", "wt"), "out"),
        P("out", ("wt", "inp")),
        P("out", ("wt", "inp")),
        P(("wt", "inp"), "out"),
        P(None, ("inp", "wt"), "out"),
    )
    out_specs = (
        P(None, ("inp", "wt"), "out"),
        P(None, ("inp", "wt"), "out"),
        P("out", ("wt", "inp")),
        P("out", ("wt", "inp")),
        P(("wt", "inp"), "out"),
    )
    return jax.shard_map(
        on_device, mesh=mesh, in_specs=in_specs, out_specs=out_specs, check_vma=False
    )
```

profile of v0, /device:TPU:0, one launch (start us, length us, event | category | flops | bytes accessed | tf_op | source)
XLA Modules:
  0.0 537.6 jit_solution(12224028123206890003)
XLA Ops:
  8.7 9.2 %all_gather.26 = bf16[256,1024]{1,0:T(8,128)(2,1)S(1)} all-gather(bf16[256,256]{1,0:T(8,128)(2,1)} %param.7), channel_id=1, replica_groups=mesh['inp'=4,'wt'=4,'out'=8] {'inp'}, dimensions={1}, use_global_device_ids=true | all-gather | bytes 655360 | tf_op jit(solution)/shard_map/all_gather | solution.py:24
  17.9 18.2 %all-gather.6.cloned.1.call-done = bf16[2,1024,256]{2,1,0:T(8,128)(2,1)} async-done(((bf16[2,256,256]{2,1,0:T(8,128)(2,1)}), bf16[2,1024,256]{2,1,0:T(8,128)(2,1)}) %all-gather.6.cloned.1.call-update) | async-done | bytes 1048592 | tf_op jit(solution)/shard_map/all_gather | solution.py:19
  36.1 4.6 convolution_convert_fusion.1
  40.7 8.7 %all_gather.25 = bf16[256,1024]{1,0:T(8,128)(2,1)S(1)} all-gather(bf16[256,256]{1,0:T(8,128)(2,1)S(1)} %copy-done.4), channel_id=1, replica_groups=mesh['inp'=4,'wt'=4,'out'=8] {'inp'}, dimensions={1}, use_global_device_ids=true | all-gather | bytes 655360 | tf_op jit(solution)/shard_map/all_gather | solution.py:23
  50.2 3.3 convolution_convert_fusion.2
  53.6 8.8 %all_gather.28 = bf16[1024,256]{1,0:T(8,128)(2,1)S(1)} all-gather(bf16[256,256]{1,0:T(8,128)(2,1)S(1)} %copy-done.5), channel_id=1, replica_groups=mesh['inp'=4,'wt'=4,'out'=8] {'inp'}, dimensions={0}, use_global_device_ids=true | all-gather | bytes 655360 | tf_op jit(solution)/shard_map/all_gather | solution.py:26
  62.5 4.5 convolution_convert_fusion
  67.1 51.1 %reduce-scatter.11.cloned.1.call-done = bf16[2,128,1024]{2,1,0:T(8,128)(2,1)} async-done(((bf16[2,1024,1024]{2,1,0:T(8,128)(2,1)}), bf16[2,128,1024]{2,1,0:T(8,128)(2,1)}) %reduce-scatter.11.cloned.1.call-update) | async-done | bytes 524304 | tf_op jit(solution)/shard_map/reduce_scatter | solution.py:34
  118.1 54.2 %reduce-scatter.9.cloned.1.call-done = bf16[2,128,1024]{2,1,0:T(8,128)(2,1)} async-done(((bf16[2,1024,1024]{2,1,0:T(8,128)(2,1)}), bf16[2,128,1024]{2,1,0:T(8,128)(2,1)}) %reduce-scatter.9.cloned.1.call-update) | async-done | bytes 524304 | tf_op jit(solution)/shard_map/reduce_scatter | solution.py:31
  172.4 54.2 %reduce-scatter.15.cloned.1.call-done = bf16[2,128,1024]{2,1,0:T(8,128)(2,1)} async-done(((bf16[2,1024,1024]{2,1,0:T(8,128)(2,1)}), bf16[2,128,1024]{2,1,0:T(8,128)(2,1)}) %reduce-scatter.15.cloned.1.call-update) | async-done | bytes 524304 | tf_op jit(solution)/shard_map/reduce_scatter | solution.py:38
  226.6 3.3 fusion.8
  231.5 50.1 %all-gather.12.cloned.1.call-done = bf16[2,1024,1024]{2,1,0:T(8,128)(2,1)} async-done(((bf16[2,128,1024]{2,1,0:T(8,128)(2,1)}), bf16[2,1024,1024]{2,1,0:T(8,128)(2,1)}) %all-gather.12.cloned.1.call-update) | async-done | bytes 4194320 | tf_op jit(solution)/shard_map/all_gather | solution.py:44
  281.6 4.3 fusion.4
  285.9 48.7 %all-gather.14.cloned.1.call-done = bf16[2,1024,1024]{2,1,0:T(8,128)(2,1)} async-done(((bf16[2,128,1024]{2,1,0:T(8,128)(2,1)}), bf16[2,1024,1024]{2,1,0:T(8,128)(2,1)}) %all-gather.14.cloned.1.call-update) | async-done | bytes 4194320 | tf_op jit(solution)/shard_map/all_gather | solution.py:45
  334.7 4.3 fusion.3
  339.1 48.7 %all-gather.8.cloned.1.call-done = bf16[2,1024,1024]{2,1,0:T(8,128)(2,1)} async-done(((bf16[2,128,1024]{2,1,0:T(8,128)(2,1)}), bf16[2,1024,1024]{2,1,0:T(8,128)(2,1)}) %all-gather.8.cloned.1.call-update) | async-done | bytes 4194320 | tf_op jit(solution)/shard_map/all_gather | solution.py:42
  387.8 4.3 fusion.2
  392.4 3.7 fusion.18
  398.6 4.5 convolution_convert_fusion.3
  403.0 14.6 %reduce-scatter.19.cloned.1.call-done = bf16[256,256]{0,1:T(8,128)(2,1)} async-done(((bf16[256,1024]{0,1:T(8,128)(2,1)}), bf16[256,256]{0,1:T(8,128)(2,1)}) %reduce-scatter.19.cloned.1.call-update) | async-done | bytes 131088 | tf_op jit(solution)/shard_map/reduce_scatter | solution.py:67
  419.3 28.9 %reduce-scatter.21.cloned.1.call-done = bf16[256,256]{0,1:T(8,128)(2,1)} async-done(((bf16[256,1024]{0,1:T(8,128)(2,1)}), bf16[256,256]{0,1:T(8,128)(2,1)}) %reduce-scatter.21.cloned.1.call-update) | async-done | bytes 131088 | tf_op jit(solution)/shard_map/reduce_scatter | solution.py:70
  449.9 28.9 %reduce-scatter.23.cloned.1.call-done = bf16[256,256]{1,0:T(8,128)(2,1)} async-done(((bf16[1024,256]{1,0:T(8,128)(2,1)}), bf16[256,256]{1,0:T(8,128)(2,1)}) %reduce-scatter.23.cloned.1.call-update) | async-done | bytes 131088 | tf_op jit(solution)/shard_map/reduce_scatter | solution.py:77
  480.5 24.3 %reduce-scatter.17.cloned.1.call-done = bf16[2,256,256]{2,1,0:T(8,128)(2,1)} async-done(((bf16[2,1024,256]{2,1,0:T(8,128)(2,1)}), bf16[2,256,256]{2,1,0:T(8,128)(2,1)}) %reduce-scatter.17.cloned.1.call-update) | async-done | bytes 262160 | tf_op jit(solution)/shard_map/reduce_scatter | solution.py:59
  504.7 26.3 %reduce-scatter.13.cloned.1.call-done = bf16[2,256,256]{2,1,0:T(8,128)(2,1)} async-done(((bf16[2,1024,256]{2,1,0:T(8,128)(2,1)}), bf16[2,256,256]{2,1,0:T(8,128)(2,1)}) %reduce-scatter.13.cloned.1.call-update) | async-done | bytes 262160 | tf_op jit(solution)/shard_map/reduce_scatter | solution.py:50
  (45 shorter events, 11.9 us)
Async XLA Ops:
  7.2 28.9 %all-gather.6.cloned.1.call-start = ((), (), s32[]{:S(2)}) async-start(), calls=%async_computation.8 | async-start | bytes 1310720 | tf_op jit(solution)/shard_map/all_gather | solution.py:19
  7.9 54.6 %all-gather.10.cloned.1.call-start = ((), (), s32[]{:S(2)}) async-start(), calls=%async_computation.13 | async-start | bytes 1310720 | tf_op jit(solution)/shard_map/all_gather | solution.py:20
  8.6 109.5 %reduce-scatter.11.cloned.1.call-start = ((), (), s32[]{:S(2)}) async-start(), calls=%async_computation.10 | async-start | bytes 4718592 | tf_op jit(solution)/shard_map/reduce_scatter | solution.py:34
  17.9 22.9 %copy-start.4 = (bf16[256,256]{1,0:T(8,128)(2,1)S(1)}, bf16[256,256]{1,0:T(8,128)(2,1)}, u32[]{:S(2)}) copy-start(bf16[256,256]{1,0:T(8,128)(2,1)} %param.6) | copy-start | bytes 393220
  36.1 14.2 %copy-start = (bf16[2,1024,256]{2,1,0:T(8,128)(2,1)S(1)}, bf16[2,1024,256]{2,1,0:T(8,128)(2,1)}, u32[]{:S(2)}) copy-start(bf16[2,1024,256]{2,1,0:T(8,128)(2,1)} %all-gather.6.cloned.1.call-done) | copy-start | bytes 3145732
  40.7 131.7 %reduce-scatter.9.cloned.1.call-start = ((), (), s32[]{:S(2)}) async-start(), calls=%async_computation.9 | async-start | bytes 4718592 | tf_op jit(solution)/shard_map/reduce_scatter | solution.py:31
  49.4 0.8 copy-start.2
  50.2 3.4 copy-start.5
  53.6 173.0 %reduce-scatter.15.cloned.1.call-start = ((), (), s32[]{:S(2)}) async-start(), calls=%async_computation.14 | async-start | bytes 4718592 | tf_op jit(solution)/shard_map/reduce_scatter | solution.py:38
  67.0 214.5 %all-gather.12.cloned.1.call-start = ((), (), s32[]{:S(2)}) async-start(), calls=%async_computation.15 | async-start | bytes 4718592 | tf_op jit(solution)/shard_map/all_gather | solution.py:44
  229.9 104.8 %all-gather.14.cloned.1.call-start = ((), (), s32[]{:S(2)}) async-start(), calls=%async_computation.16 | async-start | bytes 4718592 | tf_op jit(solution)/shard_map/all_gather | solution.py:45
  230.7 157.1 %all-gather.8.cloned.1.call-start = ((), (), s32[]{:S(2)}) async-start(), calls=%async_computation.11 | async-start | bytes 4718592 | tf_op jit(solution)/shard_map/all_gather | solution.py:42
  231.4 186.2 %reduce-scatter.19.cloned.1.call-start = ((), (), s32[]{:S(2)}) async-start(), calls=%async_computation.18 | async-start | bytes 655360 | tf_op jit(solution)/shard_map/reduce_scatter | solution.py:67
  285.9 101.9 %copy-start.1 = (bf16[2,1024,256]{2,1,0:T(8,128)(2,1)S(1)}, bf16[2,1024,256]{2,1,0:T(8,128)(2,1)}, u32[]{:S(2)}) copy-start(bf16[2,1024,256]{2,1,0:T(8,128)(2,1)} %all-gather.10.cloned.1.call-done) | copy-start | bytes 3145732
  285.9 162.3 %reduce-scatter.21.cloned.1.call-start = ((), (), s32[]{:S(2)}) async-start(), calls=%async_computation.19 | async-start | bytes 655360 | tf_op jit(solution)/shard_map/reduce_scatter | solution.py:70
  339.0 53.4 %copy-start.3 = (bf16[256,1024]{1,0:T(8,128)(2,1)S(1)}, bf16[256,1024]{1,0:T(8,128)(2,1)}, u32[]{:S(2)}) copy-start(bf16[256,1024]{1,0:T(8,128)(2,1)} %copy-done.2) | copy-start | bytes 1572868
  339.0 139.9 %reduce-scatter.23.cloned.1.call-start = ((), (), s32[]{:S(2)}) async-start(), calls=%async_computation.20 | async-start | bytes 655360 | tf_op jit(solution)/shard_map/reduce_scatter | solution.py:77
  392.1 112.6 %reduce-scatter.17.cloned.1.call-start = ((), (), s32[]{:S(2)}) async-start(), calls=%async_computation.17 | async-start | bytes 1310720 | tf_op jit(solution)/shard_map/reduce_scatter | solution.py:59
  392.4 3.7 copy-start.6
  398.5 132.5 %reduce-scatter.13.cloned.1.call-start = ((), (), s32[]{:S(2)}) async-start(), calls=%async_computation.12 | async-start | bytes 1310720 | tf_op jit(solution)/shard_map/reduce_scatter | solution.py:50
Sparse Core Ops, SparseCore 0:
  9.7 26.3 all-gather.5
  37.8 24.2 all-gather.9
  64.5 53.6 reduce-scatter.10
  120.4 51.9 reduce-scatter.8
  174.6 51.9 reduce-scatter.14
  230.0 51.4 all-gather.11
  283.2 51.4 all-gather.13
  336.3 51.4 all-gather.7
  390.4 27.1 reduce-scatter.18
  420.2 27.9 reduce-scatter.20
  450.8 27.9 reduce-scatter.22
  481.8 22.8 reduce-scatter.16
  507.7 23.2 reduce-scatter.12
where the time goes:
time: 538 us
  waiting for transfers between devices  451 us (84%)
  matrix products  35.9 us (7%)
  blocking collectives  26.7 us (5%)
  between operations  14 us (3%)
    reduce_scatter x1, waiting for transfers between devices, on_device(): lax.psum_scatter(gate_part.astype(jnp.bfloat16), 'out', scatter_dimension...  54.2 us
    reduce_scatter x1, waiting for transfers between devices, on_device(): lax.psum_scatter(back_part.astype(jnp.bfloat16), 'out', scatter_dimension...  54.2 us
    reduce_scatter x1, waiting for transfers between devices, on_device(): lax.psum_scatter(up_part.astype(jnp.bfloat16), 'out', scatter_dimension=1...  51.1 us
    all_gather x1, waiting for transfers between devices, on_device(): lax.all_gather(gate_act_own, 'out', axis=1, tiled=True)  50.1 us
    all_gather x1, waiting for transfers between devices, on_device(): hidden_rows = lax.all_gather(hidden_own, 'out', axis=1, tiled=True)  48.7 us
    all_gather x1, waiting for transfers between devices, on_device(): lax.all_gather(up_act_own, 'out', axis=1, tiled=True)  48.7 us
    reduce_scatter x1, waiting for transfers between devices, on_device(): lax.psum_scatter(down_term.astype(jnp.bfloat16), 'inp', scatter_dimension...  28.9 us
    reduce_scatter x1, waiting for transfers between devices, on_device(): lax.psum_scatter(up_term.astype(jnp.bfloat16), 'inp', scatter_dimension=1...  28.9 us
  transfers between devices with their start and end apart: 13, of which 12 were waited for; matrix products, arithmetic and copies ran while one was open for 8% of the time, Pallas kernels for 0%

commit v1 on v0

v1 whole, which is shorter than its diff:
```python
import functools

import jax
import jax.numpy as jnp
from jax import lax
from jax.experimental import pallas as pl
from jax.experimental.pallas import tpu as pltpu
from jax.sharding import PartitionSpec as P

MESH = pl.DeviceIdType.MESH
BF16 = jnp.bfloat16
F32 = jnp.float32

NN = (((1,), (0,)), ((), ()))
NT = (((1,), (1,)), ((), ()))
TN = (((0,), (0,)), ((), ()))


def dot(a, b, dims):
    return lax.dot_general(a, b, dims, preferred_element_type=F32)


class Sems:
    def __init__(self, ref, size):
        self.ref, self.size, self.used = ref, size, 0

    def take(self):
        assert self.used < self.size
        self.used += 1
        return self.ref.at[self.used - 1]


N_SEND = 128
N_RECV = 96


def kernel(
    tok, gate_w, up_w, down_w, cot,
    out_ref, gtok_ref, ggate_ref, gup_ref, gdown_ref,
    down_t, xin, wts, part_own, part_out, part_in, act, res, wgr,
    rxa0, rxa1, rxb0, rxb1, ry0, ry1, sy, fin, rza, rzb, sw, hw,
    send_sems, recv_sems, hw_in,
):
    i, x, o = lax.axis_index("inp"), lax.axis_index("wt"), lax.axis_index("out")
    h, c, l, z = i // 2, i % 2, o // 4, o % 4
    p = (h + l) % 2

    def dev(h, c, x, l, z):
        return {"inp": h * 2 + c, "wt": x, "out": l * 4 + z}

    def ring(v, d):
        return (v + d + 4) % 4

    x_to = [dev(h, c, ring(x, 1), l, z), dev(h, c, ring(x, -1), l, z)]
    z_to = [dev(h, c, x, l, ring(z, 1)), dev(h, c, x, l, ring(z, -1))]
    y_to = dev(1 - h, c, x, 1 - l, z)
    core_to = dev(h, 1 - c, x, l, z)

    sends = Sems(send_sems, N_SEND)
    recvs = Sems(recv_sems, N_RECV)
    pending = []

    def send(src, dst, sem, to):
        copy = pltpu.make_async_remote_copy(
            src, dst, sends.take(), sem, device_id=to, device_id_type=MESH
        )
        copy.start()
        pending.append(copy)

    def send_or_keep(src, dst, sem, to, mine):
        copy = pltpu.make_async_remote_copy(
            src, dst, sends.take(), sem, device_id=to, device_id_type=MESH
        )

        @pl.when(mine)
        def _():
            pltpu.make_async_copy(src, dst, sem).start()

        @pl.when(jnp.logical_not(mine))
        def _():
            copy.start()

        pending.append((copy, mine))

    def arrived(ref, sem):
        pltpu.make_async_copy(ref, ref, sem).wait()

    def rows(start, size):
        return pl.ds(pl.multiple_of(start, 64), size)

    def cols(start, size):
        return pl.ds(pl.multiple_of(start, 256), size)

    barrier = pltpu.get_barrier_semaphore()
    met = 0
    for dl in range(2):
        for dz in range(4):
            for dc in range(2):
                if dl or dz or dc:
                    to = dev(h, (c + dc) % 2, x, (l + dl) % 2, ring(z, dz))
                    pl.semaphore_signal(barrier, inc=1, device_id=to, device_id_type=MESH)
                    met += 1
    for to in x_to + [y_to]:
        pl.semaphore_signal(barrier, inc=1, device_id=to, device_id_type=MESH)
        met += 1
    down_t[...] = down_w[...].T
    pl.semaphore_wait(barrier, met)

    source = [tok, cot]
    own_slot = (x * 2 + h) * 128
    x_a2a = [recvs.take(), recvs.take()]
    w_in = [recvs.take() for _ in range(3)]
    weights = [gate_w, up_w, down_t]

    def scatter(a):
        for dl, dz in ((1, 2), (0, 2), (1, 1), (1, 3), (0, 1), (0, 3), (1, 0), (0, 0)):
            lt, zt = (l + dl) % 2, ring(z, dz)
            label = ((h + lt) % 2) * 4 + zt
            src = source[a].at[rows(label * 64, 64), :]
            dst = xin.at[a, rows(own_slot + c * 64, 64), cols(z * 256, 256)]
            to = dev(h, l, x, lt, zt)
            if dl or dz:
                send(src, dst, x_a2a[a], to)
            else:
                send_or_keep(src, dst, x_a2a[a], to, c == l)

    def spread_weight(w):
        dst = wts.at[w, rows(z * 256, 256), cols(c * 256, 256)]
        send(weights[w], dst, w_in[w], dev(h, l, x, 1 - l, z))
        send_or_keep(weights[w], dst, w_in[w], dev(h, l, x, l, z), c == l)

    scatter(1)
    spread_weight(0)
    scatter(0)
    spread_weight(1)
    spread_weight(2)

    def x_slot(a, dx, other=False, start=0, size=128):
        hh = 1 - h if other else h
        return xin.at[a, rows((ring(x, dx) * 2 + hh) * 128 + start, size), :]

    y_x0 = recvs.take()
    y_x1 = [recvs.take() for _ in range(4)]
    x_hop = {
        key: [[recvs.take(), recvs.take()], [recvs.take(), recvs.take()]]
        for key in ((1, False), (0, False), (0, True))
    }
    z_hop = [[[recvs.take(), recvs.take()], [recvs.take(), recvs.take()]] for _ in range(3)]

    def x_first(a, other):
        for d in range(2):
            ref = x_slot(a, 0, other)
            send(ref, ref, x_hop[a, other][0][d], x_to[d])

    def x_second(a, other):
        for d, dx in ((0, -1), (1, 1)):
            arrived(x_slot(a, dx, other), x_hop[a, other][0][d])
            ref = x_slot(a, dx, other, 64 * d, 64)
            send(ref, ref, x_hop[a, other][1][d], x_to[d])

    def x_last(a, other):
        for d in range(2):
            arrived(x_slot(a, 2, other, 64 * d, 64), x_hop[a, other][1][d])

    def w_block(w, dz, start=0, size=256):
        return wts.at[w, rows(ring(z, dz) * 256 + start, size), :]

    def z_first(w):
        arrived(w_block(w, 0), w_in[w])
        for d in range(2):
            send(w_block(w, 0), w_block(w, 0), z_hop[w][0][d], z_to[d])

    def z_second(w):
        for d, dz in ((0, -1), (1, 1)):
            arrived(w_block(w, dz), z_hop[w][0][d])
            ref = w_block(w, dz, 128 * d, 128)
            send(ref, ref, z_hop[w][1][d], z_to[d])

    def z_last(w):
        for d in range(2):
            arrived(w_block(w, 2, 128 * d, 128), z_hop[w][1][d])

    def y_send(dx):
        send(x_slot(1, dx), x_slot(1, dx), y_x1[dx % 4], y_to)

    z_first(0)
    arrived(x_slot(1, 0), x_a2a[1])
    x_first(1, False)
    arrived(x_slot(0, 0), x_a2a[0])
    send(x_slot(0, 0), x_slot(0, 0), y_x0, y_to)
    x_first(0, False)
    y_send(0)
    z_first(1)
    z_first(2)
    x_second(1, False)
    y_send(-1)
    y_send(1)
    arrived(x_slot(0, 0, True), y_x0)
    x_first(0, True)
    z_second(0)
    x_second(0, False)
    z_second(1)
    x_last(1, False)
    y_send(2)
    x_second(0, True)
    z_second(2)
    x_last(0, False)
    for w in range(3):
        z_last(w)

    p_in = [recvs.take() for _ in range(4)]
    a_in = [recvs.take() for _ in range(4)]

    def products(dx):
        arrived(x_slot(1, dx, True), y_x1[dx % 4])
        base = ring(x, dx) * 256
        mine, theirs = base + c * 128, base + (1 - c) * 128
        for w in range(3):
            lhs = jnp.concatenate(
                [xin[w // 2, rows(mine, 128), :], xin[w // 2, rows(theirs, 128), :]], axis=0
            )
            r = dot(lhs, wts[w], NN)
            part_own[dx % 4, w] = r[:128]
            part_out[dx % 4, w] = r[128:].astype(BF16)
        send(part_out.at[dx % 4], part_in.at[dx % 4], p_in[dx % 4], core_to)

    def activate(dx):
        g = dx % 4
        arrived(part_in.at[g], p_in[g])
        mine = ring(x, dx) * 256 + c * 128
        gate = part_own[g, 0] + part_in[g, 0].astype(F32)
        up = part_own[g, 1] + part_in[g, 1].astype(F32)
        back = part_own[g, 2] + part_in[g, 2].astype(F32)
        s = jax.nn.sigmoid(gate)
        silu = gate * s
        act[0, rows(mine, 128), :] = (back * up * (s * (1.0 + gate * (1.0 - s)))).astype(BF16)
        act[1, rows(mine, 128), :] = (back * silu).astype(BF16)
        act[2, rows(mine, 128), :] = (silu * up).astype(BF16)
        ref = act.at[:, rows(mine, 128), :]
        send(ref, ref, a_in[g], core_to)

    def act_ready(dx):
        theirs = ring(x, dx) * 256 + (1 - c) * 128
        arrived(act.at[:, rows(theirs, 128), :], a_in[dx % 4])

    products(0)
    products(1)
    activate(0)
    products(-1)
    activate(1)
    x_last(0, True)
    products(2)
    activate(-1)
    activate(2)

    def backward(dx):
        at = rows(ring(x, dx) * 256, 256)
        r = dot(act[0, at, :], wts[0], NT) + dot(act[1, at, :], wts[1], NT)
        res[1, at, :] = r.astype(BF16)
        send(r_slot(1, dx, True), ry1.at[dx % 4], ry1_in[dx % 4], y_to)
        r = dot(act[2, at, :], wts[2], NT)
        res[0, at, :] = r.astype(BF16)

    def r_group(dx, start=0, size=256):
        return res.at[0, rows(ring(x, dx) * 256 + start, size), :]

    def r_slot(a, dx, other=False, start=0, size=128):
        hh = 1 - h if other else h
        return res.at[a, rows((ring(x, dx) * 2 + hh) * 128 + start, size), :]

    def add_into(ref, inc):
        ref[...] = (ref[...].astype(F32) + inc[...].astype(F32)).astype(BF16)

    def take2():
        return [recvs.take(), recvs.take()]

    ry0_in = recvs.take()
    ry1_in = [recvs.take() for _ in range(4)]
    rxa0_in, rxa1_in, rxb0_in, rxb1_in = take2(), take2(), take2(), take2()
    rza_in = [take2() for _ in range(3)]
    rzb_in = [take2() for _ in range(3)]
    home_in = take2()

    def summed1(dx):
        arrived(ry1.at[dx % 4], ry1_in[dx % 4])
        add_into(r_slot(1, dx), ry1.at[dx % 4])

    def g_block(w, dz, start=0, size=256):
        return wgr.at[w, rows(ring(z, dz) * 256 + start, size), :]

    def weight_grads(dz):
        at = cols(ring(z, dz) * 256, 256)
        for w in range(3):
            r = dot(xin[w // 2, :, at], act[w], TN)
            g_block(w, dz)[...] = r.astype(BF16)

    def z_step1():
        for w in range(3):
            for d in range(2):
                send(g_block(w, 2, 128 * d, 128), rza.at[w, d], rza_in[w][d], z_to[d])

    def z_step2(d, dz):
        for w in range(3):
            arrived(rza.at[w, d], rza_in[w][d])
            add_into(g_block(w, dz, 128 * d, 128), rza.at[w, d])
            send(g_block(w, dz), rzb.at[w, d], rzb_in[w][d], z_to[d])

    act_ready(2)
    backward(2)
    for d in range(2):
        send(r_group(2, 128 * d, 128), rxa0.at[d], rxa0_in[d], x_to[d])
    act_ready(0)
    act_ready(1)
    act_ready(-1)
    weight_grads(2)
    z_step1()
    summed1(2)
    for d in range(2):
        send(r_slot(1, 2, False, 64 * d, 64), rxa1.at[d], rxa1_in[d], x_to[d])
    for d, dx in ((0, 1), (1, -1)):
        backward(dx)
        arrived(rxa0.at[d], rxa0_in[d])
        add_into(r_group(dx, 128 * d, 128), rxa0.at[d])
        send(r_group(dx), rxb0.at[d], rxb0_in[d], x_to[d])
        weight_grads(dx)
        z_step2(d, dx)
    for d, dx in ((0, 1), (1, -1)):
        summed1(dx)
        arrived(rxa1.at[d], rxa1_in[d])
        add_into(r_slot(1, dx, False, 64 * d, 64), rxa1.at[d])
        send(r_slot(1, dx), rxb1.at[d], rxb1_in[d], x_to[d])
    backward(0)
    weight_grads(0)
    summed1(0)

    for d in range(2):
        arrived(rxb0.at[d], rxb0_in[d])
    other = r_group(0, (1 - h) * 128, 128)
    sy[...] = (
        other[...].astype(F32)
        + rxb0[0, rows((1 - h) * 128, 128), :].astype(F32)
        + rxb0[1, rows((1 - h) * 128, 128), :].astype(F32)
    ).astype(BF16)
    send(sy, ry0, ry0_in, y_to)

    home = [out_ref, gtok_ref]

    def go_home(a):
        for dz in (2, 1, 3, 0):
            for dc in (1, 0):
                zt, ct = ring(z, dz), (c + dc) % 2
                src = fin.at[a, rows(ct * 64, 64), cols(zt * 256, 256)]
                dst = home[a].at[rows((p * 4 + z) * 64, 64), :]
                to = dev(h, ct, x, c, zt)
                if dz or dc:
                    send(src, dst, home_in[a], to)
                else:
                    send_or_keep(src, dst, home_in[a], to, c == l)

    for d in range(2):
        arrived(rxb1.at[d], rxb1_in[d])
    fin[1] = (
        r_slot(1, 0)[...].astype(F32) + rxb1[0].astype(F32) + rxb1[1].astype(F32)
    ).astype(BF16)
    go_home(1)

    for w in range(3):
        for d in range(2):
            arrived(rzb.at[w, d], rzb_in[w][d])
        sw[w] = (
            g_block(w, 0)[...].astype(F32) + rzb[w, 0].astype(F32) + rzb[w, 1].astype(F32)
        ).astype(BF16)
    for dc in (1, 0):
        ct = (c + dc) % 2
        src = sw.at[:, :, cols(ct * 256, 256)]
        to = dev(h, ct, x, c, z)
        if dc:
            send(src, hw.at[l], hw_in.at[l], to)
        else:
            send_or_keep(src, hw.at[l], hw_in.at[l], to, c == l)

    arrived(ry0, ry0_in)
    at = rows(h * 128, 128)
    fin[0] = (
        r_slot(0, 0)[...].astype(F32)
        + rxb0[0, at, :].astype(F32)
        + rxb0[1, at, :].astype(F32)
        + ry0[...].astype(F32)
    ).astype(BF16)
    go_home(0)

    for ls in range(2):
        arrived(hw.at[ls], hw_in.at[ls])
    ggate_ref[...] = hw[0, 0].astype(F32) + hw[1, 0].astype(F32)
    gup_ref[...] = hw[0, 1].astype(F32) + hw[1, 1].astype(F32)
    gdown_ref[...] = (hw[0, 2].astype(F32) + hw[1, 2].astype(F32)).T
    for a in (1, 0):
        arrived(home[a], home_in[a])

    for item in pending:
        if isinstance(item, tuple):
            copy, mine = item

            @pl.when(jnp.logical_not(mine))
            def _(copy=copy):
                copy.wait_send()
        else:
            item.wait_send()


def on_device(tokens, gate_weight, up_weight, down_weight, cotangent):
    vmem = pl.BlockSpec(memory_space=pltpu.VMEM)
    results = pl.pallas_call(
        kernel,
        name="swiglu",
        out_shape=[jax.ShapeDtypeStruct((512, 256), BF16)] * 2
        + [jax.ShapeDtypeStruct((256, 256), F32)] * 3,
        in_specs=[vmem] * 5,
        out_specs=[vmem] * 5,
        scratch_shapes=[
            pltpu.VMEM((256, 256), BF16),
            pltpu.VMEM((2, 1024, 1024), BF16),
            pltpu.VMEM((3, 1024, 512), BF16),
            pltpu.VMEM((4, 3, 128, 512), F32),
            pltpu.VMEM((4, 3, 128, 512), BF16),
            pltpu.VMEM((4, 3, 128, 512), BF16),
            pltpu.VMEM((3, 1024, 512), BF16),
            pltpu.VMEM((2, 1024, 1024), BF16),
            pltpu.VMEM((3, 1024, 512), BF16),
            pltpu.VMEM((2, 128, 1024), BF16),
            pltpu.VMEM((2, 64, 1024), BF16),
            pltpu.VMEM((2, 256, 1024), BF16),
            pltpu.VMEM((2, 128, 1024), BF16),
            pltpu.VMEM((128, 1024), BF16),
            pltpu.VMEM((4, 128, 1024), BF16),
            pltpu.VMEM((128, 1024), BF16),
            pltpu.VMEM((2, 128, 1024), BF16),
            pltpu.VMEM((3, 2, 128, 512), BF16),
            pltpu.VMEM((3, 2, 256, 512), BF16),
            pltpu.VMEM((3, 256, 512), BF16),
            pltpu.VMEM((2, 3, 256, 256), BF16),
            pltpu.SemaphoreType.DMA((N_SEND,)),
            pltpu.SemaphoreType.DMA((N_RECV,)),
            pltpu.SemaphoreType.DMA((2,)),
        ],
        compiler_params=pltpu.CompilerParams(
            collective_id=0, has_side_effects=True, vmem_limit_bytes=60 << 20
        ),
        cost_estimate=pl.CostEstimate(
            flops=9 * 2 * 1024 * 1024 * 512, bytes_accessed=3 << 20, transcendentals=1024 * 256
        ),
    )(
        tokens.reshape(512, 256),
        gate_weight,
        up_weight,
        down_weight,
        cotangent.reshape(512, 256),
    )
    output, grad_tokens, grad_gate, grad_up, grad_down = results
    return (
        output.reshape(2, 256, 256),
        grad_tokens.reshape(2, 256, 256),
        grad_gate,
        grad_up,
        grad_down,
    )


def solution(mesh):
    in_specs = (
        P(None, ("inp", "wt"), "out"),
        P("out", ("wt", "inp")),
        P("out", ("wt", "inp")),
        P(("wt", "inp"), "out"),
        P(None, ("inp", "wt"), "out"),
    )
    out_specs = (
        P(None, ("inp", "wt"), "out"),
        P(None, ("inp", "wt"), "out"),
        P("out", ("wt", "inp")),
        P("out", ("wt", "inp")),
        P(("wt", "inp"), "out"),
    )
    return jax.shard_map(
        on_device, mesh=mesh, in_specs=in_specs, out_specs=out_specs, check_vma=False
    )
```

time: 538 us -> 110 us (0.20)
  waiting for transfers between devices: 451 us -> 0 us
  Pallas kernels: 0 us -> 102 us
  matrix products: 35.9 us -> 0 us
  blocking collectives: 26.7 us -> 0 us
  between operations: 14 us -> 0.65 us
    reduce_scatter x8 -> x0, waiting for transfers between devices: 282 us -> none  [the longest x1 54.2 us: on_device(): lax.psum_scatter(gate_part.astype(jnp.bfloat16), 'out', scatter_dimension...]
    all_gather x5 -> x0, waiting for transfers between devices: 166 us -> none  [the longest x1 50.1 us: on_device(): lax.all_gather(gate_act_own, 'out', axis=1, tiled=True)]
    pallas_call x0 -> x1, Pallas kernels: none -> 102 us  [on_device(): pl.pallas_call(kernel, name='swiglu', out_shape=[jax.ShapeDtypeStruct((51...]
    dot_general x9 -> x0, matrix products: 35.9 us -> none  [the longest x1 4.57 us: on_device(): jnp.einsum('btd,df->btf', in_block, up_full, preferred_element_type=jnp.f...]
    all_gather x3 -> x0, blocking collectives: 26.7 us -> none  [the longest x1 9.17 us: on_device(): lax.all_gather(up_weight, 'inp', axis=1, tiled=True)]
  transfers between devices with their start and end apart: 13 -> 0, of which waited for: 12 -> 0; matrix products, arithmetic and copies ran while one was open for 8% -> 0% of each run, Pallas kernels for 0% -> 0%
where the time goes in v1:
time: 110 us; the launch traced here: 108 us
  Pallas kernels  102 us (93%)
  local copies, waits for them, and re-layouts  5.55 us (5%)
    pallas_call x1, Pallas kernels, on_device(): pl.pallas_call(kernel, name='swiglu', out_shape=[jax.ShapeDtypeStruct((51...  102 us
    unnamed x13, local copies, waits for them, and re-layouts  5.55 us

profile of v1, /device:TPU:0, one launch (start us, length us, event | category | flops | bytes accessed | tf_op | source)
XLA Modules:
  0.0 108.4 jit_solution(2509530020420378503)
XLA Ops:
  0.6 102.2 %swiglu.1 = (bf16[512,256]{1,0:T(8,128)(2,1)}, bf16[512,256]{1,0:T(8,128)(2,1)}, f32[256,256]{1,0:T(8,128)}, f32[256,256]{1,0:T(8,128)}, f32[256,256]{1,0:T(8,128)}) custom-call(bf16[512,256]{1,0:T(8,128)(2,1)} %bitcast.6, bf16[256,256]{1,0:T(8,128)(2,1)} %gate_w.1, bf16[256,256]{1,0:T(8,128)(2,1)} %up_w.1, bf16[256,256]{1,0:T(8,128)(2,1)} %down_w.1, ...), custom_call_target="tpu_custom_call" | custom-call | flops 9663676416 | bytes 3145728 | tf_op jit(solution)/shard_map/swiglu/pallas_call | solution.py:413
  102.8 0.0 copy-start.3
  102.8 1.7 %copy.15 = bf16[2,256,256]{2,1,0:T(8,128)(2,1)} copy(bf16[2,256,256]{2,1,0:T(8,128)(2,1)} %bitcast.5) | data formatting | bytes 524288
  104.5 0.0 copy-done.3
  104.5 0.0 copy-start.2
  104.5 0.7 copy.16
  105.2 0.3 copy-done.2
  105.6 0.0 copy-start.1
  105.6 0.7 copy.17
  106.3 0.3 copy-done.1
  106.6 0.0 copy-start
  106.6 0.7 copy.18
  107.3 0.3 copy-done
  107.7 0.7 copy.19
Async XLA Ops:
  102.8 1.7 %copy-start.3 = (bf16[512,256]{1,0:T(8,128)(2,1)S(1)}, bf16[512,256]{1,0:T(8,128)(2,1)}, u32[]{:S(2)}) copy-start(bf16[512,256]{1,0:T(8,128)(2,1)} %get-tuple-element.11) | copy-start | bytes 786436
  104.5 1.0 copy-start.2
  105.6 1.0 copy-start.1
  106.6 1.0 copy-start

commit v2 on v1

v2 whole, which is shorter than its diff:
```python
import jax
import jax.numpy as jnp
from jax import lax
from jax.experimental import pallas as pl
from jax.experimental.pallas import tpu as pltpu
from jax.sharding import PartitionSpec as P

MESH = pl.DeviceIdType.MESH
BF16 = jnp.bfloat16
F32 = jnp.float32

NN = (((1,), (0,)), ((), ()))
NT = (((1,), (1,)), ((), ()))
TN = (((0,), (0,)), ((), ()))


def dot(a, b, dims):
    return lax.dot_general(a, b, dims, preferred_element_type=F32)


class Sems:
    def __init__(self, ref, size):
        self.ref, self.size, self.used = ref, size, 0

    def take(self):
        assert self.used < self.size
        self.used += 1
        return self.ref.at[self.used - 1]


N_SEND = 256
N_RECV = 224
GATHER = (0, 1, -1, 2)


def kernel(
    tok, gate_w, up_w, down_w, cot,
    out_ref, gtok_ref, ggate_ref, gup_ref, gdown_ref,
    down_t, xin, wts, wz, part_own, part_out, part_in, act, res, wgr,
    rxa0, rxa1, rxb0, rxb1, ry0, ry1, sy, fin, rza, rzb, sw, hw, gy, gz, rza2, rzb2,
    send_sems, recv_sems, hw_in, gy_in,
):
    i, x, o = lax.axis_index("inp"), lax.axis_index("wt"), lax.axis_index("out")
    h, c, l, z = i // 2, i % 2, o // 4, o % 4
    p = (h + l) % 2

    def dev(h, c, x, l, z):
        return {"inp": h * 2 + c, "wt": x, "out": l * 4 + z}

    def ring(v, d):
        return (v + d + 4) % 4

    x_to = [dev(h, c, ring(x, 1), l, z), dev(h, c, ring(x, -1), l, z)]
    z_to = [dev(h, c, x, l, ring(z, 1)), dev(h, c, x, l, ring(z, -1))]
    y_to = dev(1 - h, c, x, 1 - l, z)
    core_to = dev(h, 1 - c, x, l, z)
    WAYS = ((0, 1), (1, -1))

    sends = Sems(send_sems, N_SEND)
    recvs = Sems(recv_sems, N_RECV)
    pending = []

    def send(src, dst, sem, to):
        copy = pltpu.make_async_remote_copy(
            src, dst, sends.take(), sem, device_id=to, device_id_type=MESH
        )
        copy.start()
        pending.append(copy)

    def send_or_keep(src, dst, sem, to, mine):
        copy = pltpu.make_async_remote_copy(
            src, dst, sends.take(), sem, device_id=to, device_id_type=MESH
        )

        @pl.when(mine)
        def _():
            pltpu.make_async_copy(src, dst, sem).start()

        @pl.when(jnp.logical_not(mine))
        def _():
            copy.start()

        pending.append((copy, mine))

    def arrived(ref, sem):
        pltpu.make_async_copy(ref, ref, sem).wait()

    def rows(start, size):
        return pl.ds(pl.multiple_of(start, 64), size)

    def cols(start, size):
        return pl.ds(pl.multiple_of(start, 256), size)

    def take(n):
        return [recvs.take() for _ in range(n)]

    def add_into(ref, inc):
        ref[...] = (ref[...].astype(F32) + inc[...].astype(F32)).astype(BF16)

    barrier = pltpu.get_barrier_semaphore()
    met = 0
    for dl in range(2):
        for dz in range(4):
            for dc in range(2):
                if dl or dz or dc:
                    to = dev(h, (c + dc) % 2, x, (l + dl) % 2, ring(z, dz))
                    pl.semaphore_signal(barrier, inc=1, device_id=to, device_id_type=MESH)
                    met += 1
    for to in x_to + [y_to]:
        pl.semaphore_signal(barrier, inc=1, device_id=to, device_id_type=MESH)
        met += 1
    down_t[...] = down_w[...].T
    pl.semaphore_wait(barrier, met)

    source = [tok, cot]
    x_a2a = [take(4), take(4)]
    y0_in = take(4)
    y1_in = [take(4) for _ in range(4)]
    x_hop = {key: [[take(2), take(2)] for _ in range(4)] for key in ((1, 0), (0, 0), (0, 1))}
    w_in = [take(1), take(1), take(4)]
    z_hop = [[take(2), take(2)] for _ in range(3)]

    def x_slot(a, k, dx, other=0, start=0, size=128):
        hh = 1 - h if other else h
        return xin.at[a, ring(z, k), rows((ring(x, dx) * 2 + hh) * 128 + start, size), :]

    def scatter(a, dz):
        for dl in (1, 0):
            lt, zt = (l + dl) % 2, ring(z, dz)
            label = ((h + lt) % 2) * 4 + zt
            src = source[a].at[rows(label * 64, 64), :]
            dst = xin.at[a, z, rows((x * 2 + h) * 128 + c * 64, 64), :]
            to = dev(h, l, x, lt, zt)
            if dl or dz:
                send(src, dst, x_a2a[a][-dz % 4], to)
            else:
                send_or_keep(src, dst, x_a2a[a][0], to, c == l)

    def w_block(w, k, start=0, size=256):
        return wts.at[w, rows(ring(z, k) * 256 + start, size), :]

    def spread(w, src, k):
        dst = wts.at[w, rows(ring(z, k) * 256, 256), cols(c * 256, 256)]
        send(src, dst, w_in[w][k % 4], dev(h, l, x, 1 - l, z))
        send_or_keep(src, dst, w_in[w][k % 4], dev(h, l, x, l, z), c == l)

    def to_slot(k):
        arrived(x_slot(1, k, 0), x_a2a[1][k % 4])
        x_first(1, 0, k)
        y1_send(k, 0)
        arrived(x_slot(0, k, 0), x_a2a[0][k % 4])
        send(x_slot(0, k, 0), x_slot(0, k, 0), y0_in[k % 4], y_to)
        x_first(0, 0, k)

    def y1_send(k, dx):
        send(x_slot(1, k, dx), x_slot(1, k, dx), y1_in[k % 4][dx % 4], y_to)

    def x_first(a, other, k):
        for d in range(2):
            ref = x_slot(a, k, 0, other)
            send(ref, ref, x_hop[a, other][k % 4][0][d], x_to[d])

    def x_second(a, other, k):
        for d, dx in ((0, -1), (1, 1)):
            arrived(x_slot(a, k, dx, other), x_hop[a, other][k % 4][0][d])
            ref = x_slot(a, k, dx, other, 64 * d, 64)
            send(ref, ref, x_hop[a, other][k % 4][1][d], x_to[d])
            if a == 1:
                y1_send(k, dx)

    def x_last(a, other, k):
        for d in range(2):
            arrived(x_slot(a, k, 2, other, 64 * d, 64), x_hop[a, other][k % 4][1][d])
        if a == 1:
            y1_send(k, 2)

    def x_other(k):
        arrived(x_slot(0, k, 0, 1), y0_in[k % 4])
        x_first(0, 1, k)

    def z_first(w):
        arrived(w_block(w, 0), w_in[w][0])
        for d in range(2):
            send(w_block(w, 0), w_block(w, 0), z_hop[w][0][d], z_to[d])

    def z_second(w):
        for d, dz in ((0, -1), (1, 1)):
            arrived(w_block(w, dz), z_hop[w][0][d])
            ref = w_block(w, dz, 128 * d, 128)
            send(ref, ref, z_hop[w][1][d], z_to[d])

    def z_last(w):
        for d in range(2):
            arrived(w_block(w, 2, 128 * d, 128), z_hop[w][1][d])

    def d_first():
        for d in range(2):
            send(down_t, wz.at[z], z_hop[2][0][d], z_to[d])
        spread(2, down_t, 0)

    def d_second():
        for d, dz in ((0, -1), (1, 1)):
            at = ring(z, dz)
            arrived(wz.at[at], z_hop[2][0][d])
            ref = wz.at[at, rows(128 * d, 128), :]
            send(ref, ref, z_hop[2][1][d], z_to[d])
            spread(2, wz.at[at], dz)

    def d_last():
        at = ring(z, 2)
        for d in range(2):
            arrived(wz.at[at, rows(128 * d, 128), :], z_hop[2][1][d])
        spread(2, wz.at[at], 2)

    scatter(1, 0)
    scatter(0, 0)
    spread(0, gate_w, 0)
    for dz in (1, -1):
        scatter(1, dz)
    for dz in (1, -1):
        scatter(0, dz)
    spread(1, up_w, 0)
    scatter(1, 2)
    scatter(0, 2)
    d_first()

    to_slot(0)
    z_first(0)
    to_slot(1)
    to_slot(-1)
    z_first(1)
    x_second(1, 0, 0)
    x_second(0, 0, 0)
    x_other(0)
    to_slot(2)
    d_second()
    x_last(1, 0, 0)
    x_second(0, 1, 0)
    z_second(0)
    for k in (1, -1):
        x_second(1, 0, k)
        x_second(0, 0, k)
        x_other(k)
    z_second(1)
    for k in (1, -1):
        x_last(1, 0, k)
        x_second(0, 1, k)
    d_last()
    x_second(1, 0, 2)
    x_second(0, 0, 2)
    x_other(2)
    x_last(1, 0, 2)
    x_second(0, 1, 2)
    for k in GATHER:
        x_last(0, 0, k)
    z_last(0)
    z_last(1)
    for k in GATHER:
        arrived(w_block(2, k), w_in[2][k % 4])
        x_last(0, 1, k)

    p_in = take(4)
    a_in = take(4)

    def products(dx):
        for k in GATHER:
            arrived(x_slot(1, k, dx, 1), y1_in[k % 4][dx % 4])
        base = ring(x, dx) * 256
        for w in range(3):
            lhs = jnp.concatenate(
                [
                    jnp.concatenate(
                        [xin[w // 2, q, rows(base + hh * 128, 128), :] for q in range(4)], axis=1
                    )
                    for hh in (c, 1 - c)
                ],
                axis=0,
            )
            r = dot(lhs, wts[w], NN)
            part_own[dx % 4, w] = r[:128]
            part_out[dx % 4, w] = r[128:].astype(BF16)
        send(part_out.at[dx % 4], part_in.at[dx % 4], p_in[dx % 4], core_to)

    def activate(dx):
        g = dx % 4
        arrived(part_in.at[g], p_in[g])
        mine = ring(x, dx) * 256 + c * 128
        gate = part_own[g, 0] + part_in[g, 0].astype(F32)
        up = part_own[g, 1] + part_in[g, 1].astype(F32)
        back = part_own[g, 2] + part_in[g, 2].astype(F32)
        s = jax.nn.sigmoid(gate)
        silu = gate * s
        act[0, rows(mine, 128), :] = (back * up * (s * (1.0 + gate * (1.0 - s)))).astype(BF16)
        act[1, rows(mine, 128), :] = (back * silu).astype(BF16)
        act[2, rows(mine, 128), :] = (silu * up).astype(BF16)
        ref = act.at[:, rows(mine, 128), :]
        send(ref, ref, a_in[g], core_to)

    def act_ready(dx):
        theirs = ring(x, dx) * 256 + (1 - c) * 128
        arrived(act.at[:, rows(theirs, 128), :], a_in[dx % 4])

    products(0)
    products(1)
    activate(0)
    products(-1)
    activate(1)
    products(2)
    activate(-1)
    activate(2)

    ry0_in = take(4)
    ry1_in = [take(4) for _ in range(4)]
    rxa0_in, rxa1_in, rxb0_in, rxb1_in = ([take(2) for _ in range(4)] for _ in range(4))
    home_in = take(2)
    rza_in = [take(2) for _ in range(2)]
    rzb_in = [take(2) for _ in range(2)]
    rza2_in, rzb2_in = take(2), take(2)

    def r_group(k, dx, start=0, size=256):
        return res.at[0, ring(z, k), rows(ring(x, dx) * 256 + start, size), :]

    def r_slot(a, k, dx, other=0, start=0, size=128):
        hh = 1 - h if other else h
        return res.at[a, ring(z, k), rows((ring(x, dx) * 2 + hh) * 128 + start, size), :]

    def backward(k, dx):
        at = rows(ring(x, dx) * 256, 256)
        r = dot(act[0, at, :], w_block(0, k)[...], NT) + dot(act[1, at, :], w_block(1, k)[...], NT)
        res[1, ring(z, k), at, :] = r.astype(BF16)
        send(r_slot(1, k, dx, 1), ry1.at[k % 4, dx % 4], ry1_in[k % 4][dx % 4], y_to)
        r = dot(act[2, at, :], w_block(2, k)[...], NT)
        res[0, ring(z, k), at, :] = r.astype(BF16)

    def step1(k):
        backward(k, 2)
        for d in range(2):
            send(r_group(k, 2, 128 * d, 128), rxa0.at[k % 4, d], rxa0_in[k % 4][d], x_to[d])

    def step2(k):
        for d, dx in WAYS:
            arrived(rxa0.at[k % 4, d], rxa0_in[k % 4][d])
            add_into(r_group(k, dx, 128 * d, 128), rxa0.at[k % 4, d])
            send(r_group(k, dx), rxb0.at[k % 4, d], rxb0_in[k % 4][d], x_to[d])

    def y_sum(k, dx):
        arrived(ry1.at[k % 4, dx % 4], ry1_in[k % 4][dx % 4])
        add_into(r_slot(1, k, dx), ry1.at[k % 4, dx % 4])

    def slot1(k):
        y_sum(k, 2)
        for d in range(2):
            send(r_slot(1, k, 2, 0, 64 * d, 64), rxa1.at[k % 4, d], rxa1_in[k % 4][d], x_to[d])

    def slot2(k):
        for d, dx in WAYS:
            y_sum(k, dx)
            arrived(rxa1.at[k % 4, d], rxa1_in[k % 4][d])
            add_into(r_slot(1, k, dx, 0, 64 * d, 64), rxa1.at[k % 4, d])
            send(r_slot(1, k, dx), rxb1.at[k % 4, d], rxb1_in[k % 4][d], x_to[d])

    home = [out_ref, gtok_ref]

    def go_home(a, k):
        for dc in (1, 0):
            ct = (c + dc) % 2
            src = fin.at[a, k % 4, rows(ct * 64, 64), :]
            dst = home[a].at[rows((p * 4 + z) * 64, 64), :]
            to = dev(h, ct, x, c, ring(z, k))
            if k or dc:
                send(src, dst, home_in[a], to)
            else:
                send_or_keep(src, dst, home_in[a], to, c == l)

    def step3(k):
        for d in range(2):
            arrived(rxb0.at[k % 4, d], rxb0_in[k % 4][d])
        at = rows((1 - h) * 128, 128)
        sy[k % 4] = (
            r_slot(0, k, 0, 1)[...].astype(F32)
            + rxb0[k % 4, 0, at, :].astype(F32)
            + rxb0[k % 4, 1, at, :].astype(F32)
        ).astype(BF16)
        send(sy.at[k % 4], ry0.at[k % 4], ry0_in[k % 4], y_to)

    def step4(k):
        arrived(ry0.at[k % 4], ry0_in[k % 4])
        at = rows(h * 128, 128)
        fin[0, k % 4] = (
            r_slot(0, k, 0)[...].astype(F32)
            + rxb0[k % 4, 0, at, :].astype(F32)
            + rxb0[k % 4, 1, at, :].astype(F32)
            + ry0[k % 4].astype(F32)
        ).astype(BF16)
        go_home(0, k)

    def slot3(k):
        arrived(ry1.at[k % 4, 0], ry1_in[k % 4][0])
        for d in range(2):
            arrived(rxb1.at[k % 4, d], rxb1_in[k % 4][d])
        fin[1, k % 4] = (
            r_slot(1, k, 0)[...].astype(F32)
            + ry1[k % 4, 0].astype(F32)
            + rxb1[k % 4, 0].astype(F32)
            + rxb1[k % 4, 1].astype(F32)
        ).astype(BF16)
        go_home(1, k)

    def g_block(w, k, start=0, size=256):
        return wgr.at[w, rows(ring(z, k) * 256 + start, size), :]

    def weight_grad(w, k):
        r = dot(xin[w // 2, ring(z, k)], act[w], TN)
        g_block(w, k)[...] = r.astype(BF16)

    def grad1(w):
        weight_grad(w, 2)
        for d in range(2):
            send(g_block(w, 2, 128 * d, 128), rza.at[w, d], rza_in[w][d], z_to[d])

    def grad2(w):
        for d, dz in WAYS:
            weight_grad(w, dz)
            arrived(rza.at[w, d], rza_in[w][d])
            add_into(g_block(w, dz, 128 * d, 128), rza.at[w, d])
            send(g_block(w, dz), rzb.at[w, d], rzb_in[w][d], z_to[d])

    def grad3(w):
        weight_grad(w, 0)
        for d in range(2):
            arrived(rzb.at[w, d], rzb_in[w][d])
        sw[w] = (
            g_block(w, 0)[...].astype(F32) + rzb[w, 0].astype(F32) + rzb[w, 1].astype(F32)
        ).astype(BF16)
        for dc in (1, 0):
            ct = (c + dc) % 2
            src = sw.at[w, :, cols(ct * 256, 256)]
            to = dev(h, ct, x, c, z)
            if dc:
                send(src, hw.at[w, l], hw_in.at[w * 2 + l], to)
            else:
                send_or_keep(src, hw.at[w, l], hw_in.at[w * 2 + l], to, c == l)

    def down1(k):
        weight_grad(2, k)
        at = ring(z, k)
        for dc in (1, 0):
            ct = (c + dc) % 2
            src = wgr.at[2, rows(at * 256, 256), cols(ct * 256, 256)]
            sem = gy_in.at[(k % 4) * 2 + l]
            to = dev(h, ct, x, c, z)
            if dc:
                send(src, gy.at[l, at], sem, to)
            else:
                send_or_keep(src, gy.at[l, at], sem, to, c == l)

    def down_sum(k):
        at = ring(z, k)
        for ls in range(2):
            arrived(gy.at[ls, at], gy_in.at[(k % 4) * 2 + ls])
        gz[at] = (gy[0, at].astype(F32) + gy[1, at].astype(F32)).astype(BF16)

    def down2():
        down_sum(2)
        for d in range(2):
            ref = gz.at[ring(z, 2), rows(128 * d, 128), :]
            send(ref, rza2.at[d], rza2_in[d], z_to[d])

    def down3():
        for d, dz in WAYS:
            down_sum(dz)
            arrived(rza2.at[d], rza2_in[d])
            add_into(gz.at[ring(z, dz), rows(128 * d, 128), :], rza2.at[d])
            send(gz.at[ring(z, dz)], rzb2.at[d], rzb2_in[d], z_to[d])

    def down4():
        down_sum(0)
        for d in range(2):
            arrived(rzb2.at[d], rzb2_in[d])
        r = gz[z].astype(F32) + rzb2[0].astype(F32) + rzb2[1].astype(F32)
        gdown_ref[...] = r.T

    act_ready(0)
    act_ready(1)
    backward(2, 1)
    act_ready(-1)
    backward(2, -1)
    act_ready(2)
    step1(2)
    grad1(0)
    backward(2, 0)
    for k in (2, 1, -1, 0):
        down1(k)
    step1(1)
    slot1(2)
    step2(2)
    grad1(1)
    backward(1, 1)
    backward(1, -1)
    grad2(0)
    slot2(2)
    backward(1, 0)
    step1(-1)
    slot1(1)
    step3(2)
    step2(1)
    down2()
    backward(-1, 1)
    backward(-1, -1)
    slot3(2)
    slot2(1)
    backward(-1, 0)
    grad2(1)
    step4(2)
    step1(0)
    slot1(-1)
    step3(1)
    step2(-1)
    backward(0, 1)
    backward(0, -1)
    down3()
    slot3(1)
    grad3(0)
    slot2(-1)
    backward(0, 0)
    step4(1)
    slot1(0)
    step3(-1)
    step2(0)
    slot3(-1)
    grad3(1)
    slot2(0)
    step4(-1)
    step3(0)
    down4()
    slot3(0)
    step4(0)

    for w, ref in ((0, ggate_ref), (1, gup_ref)):
        for ls in range(2):
            arrived(hw.at[w, ls], hw_in.at[w * 2 + ls])
        ref[...] = hw[w, 0].astype(F32) + hw[w, 1].astype(F32)
    for a in (1, 0):
        arrived(home[a], home_in[a])

    for item in pending:
        if isinstance(item, tuple):
            copy, mine = item

            @pl.when(jnp.logical_not(mine))
            def _(copy=copy):
                copy.wait_send()
        else:
            item.wait_send()


def place(*refs):
    for src, dst in zip(refs[:5], refs[5:]):
        dst[...] = src[...]


def on_device(tokens, gate_weight, up_weight, down_weight, cotangent):
    vmem = pl.BlockSpec(memory_space=pltpu.VMEM)
    shapes = [jax.ShapeDtypeStruct((512, 256), BF16)] * 2
    shapes += [jax.ShapeDtypeStruct((256, 256), F32)] * 3
    results = pl.pallas_call(
        kernel,
        name="swiglu",
        out_shape=shapes,
        in_specs=[vmem] * 5,
        out_specs=[vmem] * 5,
        scratch_shapes=[
            pltpu.VMEM((256, 256), BF16),
            pltpu.VMEM((2, 4, 1024, 256), BF16),
            pltpu.VMEM((3, 1024, 512), BF16),
            pltpu.VMEM((4, 256, 256), BF16),
            pltpu.VMEM((4, 3, 128, 512), F32),
            pltpu.VMEM((4, 3, 128, 512), BF16),
            pltpu.VMEM((4, 3, 128, 512), BF16),
            pltpu.VMEM((3, 1024, 512), BF16),
            pltpu.VMEM((2, 4, 1024, 256), BF16),
            pltpu.VMEM((3, 1024, 512), BF16),
            pltpu.VMEM((4, 2, 128, 256), BF16),
            pltpu.VMEM((4, 2, 64, 256), BF16),
            pltpu.VMEM((4, 2, 256, 256), BF16),
            pltpu.VMEM((4, 2, 128, 256), BF16),
            pltpu.VMEM((4, 128, 256), BF16),
            pltpu.VMEM((4, 4, 128, 256), BF16),
            pltpu.VMEM((4, 128, 256), BF16),
            pltpu.VMEM((2, 4, 128, 256), BF16),
            pltpu.VMEM((2, 2, 128, 512), BF16),
            pltpu.VMEM((2, 2, 256, 512), BF16),
            pltpu.VMEM((2, 256, 512), BF16),
            pltpu.VMEM((2, 2, 256, 256), BF16),
            pltpu.VMEM((2, 4, 256, 256), BF16),
            pltpu.VMEM((4, 256, 256), BF16),
            pltpu.VMEM((2, 128, 256), BF16),
            pltpu.VMEM((2, 256, 256), BF16),
            pltpu.SemaphoreType.DMA((N_SEND,)),
            pltpu.SemaphoreType.DMA((N_RECV,)),
            pltpu.SemaphoreType.DMA((4,)),
            pltpu.SemaphoreType.DMA((8,)),
        ],
        compiler_params=pltpu.CompilerParams(
            collective_id=0, has_side_effects=True, vmem_limit_bytes=60 << 20
        ),
        cost_estimate=pl.CostEstimate(
            flops=9 * 2 * 1024 * 1024 * 512, bytes_accessed=3 << 20, transcendentals=1024 * 256
        ),
    )(
        tokens.reshape(512, 256),
        gate_weight,
        up_weight,
        down_weight,
        cotangent.reshape(512, 256),
    )
    output, grad_tokens, grad_gate, grad_up, grad_down = pl.pallas_call(
        place, name="place", out_shape=shapes, in_specs=[vmem] * 5, out_specs=[vmem] * 5
    )(*results)
    return (
        output.reshape(2, 256, 256),
        grad_tokens.reshape(2, 256, 256),
        grad_gate,
        grad_up,
        grad_down,
    )


def solution(mesh):
    in_specs = (
        P(None, ("inp", "wt"), "out"),
        P("out", ("wt", "inp")),
        P("out", ("wt", "inp")),
        P(("wt", "inp"), "out"),
        P(None, ("inp", "wt"), "out"),
    )
    out_specs = (
        P(None, ("inp", "wt"), "out"),
        P(None, ("inp", "wt"), "out"),
        P("out", ("wt", "inp")),
        P("out", ("wt", "inp")),
        P(("wt", "inp"), "out"),
    )
    return jax.shard_map(
        on_device, mesh=mesh, in_specs=in_specs, out_specs=out_specs, check_vma=False
    )
```

time: 110 us -> 97.5 us (0.89)
  Pallas kernels: 102 us -> 96.3 us
  local copies, waits for them, and re-layouts: 5.55 us -> 0 us
    pallas_call x1 -> x2, Pallas kernels: 102 us -> 96.3 us  [the longest x1 94 us: on_device(): pl.pallas_call(kernel, name='swiglu', out_shape=shapes, in_specs=[vmem] *...]
    unnamed x13 -> x0, local copies, waits for them, and re-layouts: 5.55 us -> none
where the time goes in v2:
time: 97.5 us; the launch traced here: 97 us
  Pallas kernels  96.3 us (99%)
    pallas_call x1, Pallas kernels, on_device(): pl.pallas_call(kernel, name='swiglu', out_shape=shapes, in_specs=[vmem] *...  94 us
    pallas_call x1, Pallas kernels, on_device(): pl.pallas_call(place, name='place', out_shape=shapes, in_specs=[vmem] * 5...  2.33 us

profile of v2, /device:TPU:0, one launch (start us, length us, event | category | flops | bytes accessed | tf_op | source)
XLA Modules:
  0.0 97.0 jit_solution(1670971181804670656)
XLA Ops:
  0.6 94.0 %swiglu.1 = (bf16[512,256]{1,0:T(8,128)(2,1)}, bf16[512,256]{1,0:T(8,128)(2,1)}, f32[256,256]{1,0:T(8,128)}, f32[256,256]{1,0:T(8,128)}, f32[256,256]{1,0:T(8,128)}) custom-call(bf16[512,256]{1,0:T(8,128)(2,1)} %bitcast.4, bf16[256,256]{1,0:T(8,128)(2,1)} %gate_w.1, bf16[256,256]{1,0:T(8,128)(2,1)} %up_w.1, bf16[256,256]{1,0:T(8,128)(2,1)} %down_w.1, ...), custom_call_target="tpu_custom_call" | custom-call | flops 9663676416 | bytes 3145728 | tf_op jit(solution)/shard_map/swiglu/pallas_call | solution.py:566
  94.6 2.3 %place.1 = (bf16[512,256]{1,0:T(8,128)(2,1)}, bf16[512,256]{1,0:T(8,128)(2,1)}, f32[256,256]{1,0:T(8,128)}, f32[256,256]{1,0:T(8,128)}, f32[256,256]{1,0:T(8,128)}) custom-call(bf16[512,256]{1,0:T(8,128)(2,1)} %get-tuple-element.15.refs_0_, bf16[512,256]{1,0:T(8,128)(2,1)} %get-tuple-element.16.refs_1_, f32[256,256]{1,0:T(8,128)} %get-tuple-element.17.refs_2_, ...), custom_call_target="tpu_custom_call" | custom-call | tf_op jit(solution)/shard_map/place/pallas_call | solution.py:617

commit v3 on v0

v3 whole, which is shorter than its diff:
```python
import jax
import jax.numpy as jnp
from jax import lax
from jax.experimental import pallas as pl
from jax.experimental.pallas import tpu as pltpu
from jax.sharding import PartitionSpec as P

MESH = pl.DeviceIdType.MESH
BF16 = jnp.bfloat16
F32 = jnp.float32

NN = (((1,), (0,)), ((), ()))
NT = (((1,), (1,)), ((), ()))
TN = (((0,), (0,)), ((), ()))


def dot(a, b, dims):
    return lax.dot_general(a, b, dims, preferred_element_type=F32)


class Sems:
    def __init__(self, ref, size):
        self.ref, self.size, self.used = ref, size, 0

    def take(self, n=None):
        start = self.used
        self.used += n or 1
        assert self.used <= self.size
        return [self.ref.at[start + j] for j in range(n)] if n else self.ref.at[start]


N_SEND = 80
N_RECV = 150
GATHER = (0, 1, 3, 2)
FROM = ((0, 3), (1, 1))
TO = ((0, 1), (1, 3))


def kernel(
    tok, gate_w, up_w, down_w, cot,
    out_ref, gtok_ref, ggate_ref, gup_ref, gdown_ref,
    down_in, xin, wts, part, act, res, wgr, wgo, wgi,
    rxa0, rxa1, rxb0, rxb1, ry0, ry1, sy, fin, rza, rzb, gy, gl, rza2, rzb2, gy2,
    send_sems, recv_sems, own_sem,
):
    i, x, o = lax.axis_index("inp"), lax.axis_index("wt"), lax.axis_index("out")
    h, c, l, z = i // 2, i % 2, o // 4, o % 4
    p = (h + l) % 2

    def dev(h, c, x, l, z):
        return {"inp": h * 2 + c, "wt": x, "out": l * 4 + z}

    def ring(v, d):
        return (v + d) % 4

    x_to = [dev(h, c, ring(x, 1), l, z), dev(h, c, ring(x, 3), l, z)]
    z_to = [dev(h, c, x, l, ring(z, 1)), dev(h, c, x, l, ring(z, 3))]
    y_to = dev(1 - h, c, x, 1 - l, z)
    l_to = dev(h, c, x, 1 - l, z)
    core_to = dev(h, 1 - c, x, l, z)

    recvs = Sems(recv_sems, N_RECV)
    take = recvs.take
    pool = [None] * N_SEND
    count = [0]

    def send(src, dst, sem, to):
        n = count[0] % N_SEND
        count[0] += 1
        if pool[n] is not None:
            pool[n].wait_send()
        pool[n] = pltpu.make_async_remote_copy(
            src, dst, send_sems.at[n], sem, device_id=to, device_id_type=MESH
        )
        pool[n].start()

    def keep(src, dst, sem):
        pltpu.make_async_copy(src, dst, sem).start()

    def arrived(ref, sem):
        pltpu.make_async_copy(ref, ref, sem).wait()

    def rows(start, size):
        return pl.ds(pl.multiple_of(start, 64), size)

    def add_into(ref, inc):
        ref[...] = (ref[...].astype(F32) + inc[...].astype(F32)).astype(BF16)

    fetch = pltpu.make_async_copy(down_w, down_in, own_sem)
    fetch.start()
    barrier = pltpu.get_barrier_semaphore()
    partners = [dev(h, c, x, (l + dl) % 2, ring(z, dz)) for dl in range(2) for dz in range(4)][1:]
    partners += x_to + [y_to, core_to]
    for to in partners:
        pl.semaphore_signal(barrier, inc=1, device_id=to, device_id_type=MESH)
    fetch.wait()
    wts[2, c, l, 0] = down_in[...].T
    pl.semaphore_wait(barrier, len(partners))

    source = [tok, cot]
    a2a_in = [take(4), take(4)]
    x_hop = {(a, r, k): [take(2), take()] for k in range(4) for a, r in ((1, 0), (0, 0), (0, 1))}
    y0_in, y1_in = take(4), take(4)
    w_in = [take(1), take(1), take(4)]
    z_hop = [[take(2), take()] for _ in range(3)]
    pass_in = [take(4) for _ in range(3)]

    def x_slot(a, k, g, r=0, start=0, size=64):
        return xin.at[a, :, k, r, pl.ds(g * 64 + start, size), :]

    def scatter(a, dz):
        k = -dz % 4
        for dl in (1, 0):
            lt, zt = (l + dl) % 2, ring(z, dz)
            src = source[a].at[rows((((h + lt) % 2) * 4 + zt) * 64, 64), :]
            dst = xin.at[a, l, k, 0, pl.ds(0, 64), :]
            if dl or dz:
                send(src, dst, a2a_in[a][k], dev(h, c, x, lt, zt))
            else:
                keep(src, dst, a2a_in[a][k])

    def x_first(a, r, k):
        for d, g in FROM:
            send(x_slot(a, k, 0, r), x_slot(a, k, g, r), x_hop[a, r, k][0][d], x_to[d])

    def y1_send(k, g):
        send(x_slot(1, k, g), x_slot(1, k, g, 1), y1_in[k], y_to)

    def cot_in(k):
        arrived(x_slot(1, k, 0), a2a_in[1][k])
        x_first(1, 0, k)
        y1_send(k, 0)

    def tok_in(k):
        arrived(x_slot(0, k, 0), a2a_in[0][k])
        send(x_slot(0, k, 0), x_slot(0, k, 0, 1), y0_in[k], y_to)
        x_first(0, 0, k)

    def tok_other(k):
        arrived(x_slot(0, k, 0, 1), y0_in[k])
        x_first(0, 1, k)

    def x_second(a, r, k, d):
        g = FROM[d][1]
        arrived(x_slot(a, k, g, r), x_hop[a, r, k][0][d])
        half = (32 * d, 32)
        send(x_slot(a, k, g, r, *half), x_slot(a, k, 2, r, *half), x_hop[a, r, k][1], x_to[d])
        if a == 1:
            y1_send(k, g)

    def x_last(k):
        arrived(x_slot(1, k, 2), x_hop[1, 0, k][1])
        y1_send(k, 2)

    def gathered(k):
        for r in range(2):
            arrived(x_slot(0, k, 2, r), x_hop[0, r, k][1])
        arrived(xin.at[1, :, k, 1], y1_in[k])

    def w_blocks(w, k, start=0, size=256):
        return wts.at[w, c, :, k, pl.ds(start, size), :]

    def w_own(w):
        src, dst = [gate_w, up_w][w], wts.at[w, c, l, 0]
        send(src, dst, w_in[w][0], l_to)
        keep(src, dst, w_in[w][0])

    def w_pass(w, k):
        send(w_blocks(w, k), w_blocks(w, k), pass_in[w][k], core_to)

    def z_first(w):
        arrived(w_blocks(w, 0), w_in[w][0])
        for d, k in FROM:
            send(w_blocks(w, 0), w_blocks(w, k), z_hop[w][0][d], z_to[d])
        w_pass(w, 0)

    def z_second(w, d):
        k = FROM[d][1]
        arrived(w_blocks(w, k), z_hop[w][0][d])
        half = (128 * d, 128)
        send(w_blocks(w, k, *half), w_blocks(w, 2, *half), z_hop[w][1], z_to[d])
        w_pass(w, k)

    def z_last(w):
        arrived(w_blocks(w, 2), z_hop[w][1])
        w_pass(w, 2)

    def d_block(k, start=0, size=256):
        return wts.at[2, c, l, k, pl.ds(start, size), :]

    def d_first():
        for d, k in FROM:
            send(d_block(0), d_block(k), z_hop[2][0][d], z_to[d])
        send(d_block(0), d_block(0), w_in[2][0], l_to)

    def d_second(d):
        k = FROM[d][1]
        arrived(d_block(k), z_hop[2][0][d])
        half = (128 * d, 128)
        send(d_block(k, *half), d_block(2, *half), z_hop[2][1], z_to[d])
        send(d_block(k), d_block(k), w_in[2][k], l_to)

    def d_last():
        arrived(d_block(2), z_hop[2][1])
        send(d_block(2), d_block(2), w_in[2][2], l_to)

    def d_pass(k):
        arrived(wts.at[2, c, 1 - l, k], w_in[2][k])
        w_pass(2, k)

    def weight_ready(w, k):
        arrived(wts.at[w, 1 - c, :, k], pass_in[w][k])

    early = [(q, k) for q in range(2) for k in GATHER[:3]]
    late = [(q, GATHER[3]) for q in range(2)]

    def product(w, f, blocks):
        lhs = jnp.concatenate([xin[w // 2, q, k].reshape(512, 256) for q, k in blocks], axis=1)
        rhs = jnp.concatenate([wts[w, f, q, k] for q, k in blocks], axis=0)
        return dot(lhs, rhs, NN)

    def products(w):
        for f in range(2):
            part[w, f] = product(w, f, early)

    def activate(f):
        gate = part[0, f] + product(0, f, late)
        up = part[1, f] + product(1, f, late)
        back = part[2, f] + product(2, f, late)
        s = jax.nn.sigmoid(gate)
        silu = gate * s
        act[0, f] = (back * up * (s * (1.0 + gate * (1.0 - s)))).astype(BF16)
        act[1, f] = (back * silu).astype(BF16)
        act[2, f] = (silu * up).astype(BF16)

    ry0_in, ry1_in, rxb0_in, rxb1_in = (take(4) for _ in range(4))
    rxa0_in, rxa1_in = ([take(2) for _ in range(4)] for _ in range(2))
    home_in = take(2)

    def backward(w, q, k):
        lhs = jnp.concatenate([act[w, 0], act[w, 1]], axis=1)
        return dot(lhs, jnp.concatenate([wts[w, 0, q, k], wts[w, 1, q, k]], axis=1), NT)

    def slot0(k):
        for q in range(2):
            r = backward(0, q, k) + backward(1, q, k)
            res[1, q, k] = r.astype(BF16).reshape(2, 256, 256)
        send(res.at[1, :, k, 1], ry1.at[:, k], ry1_in[k], y_to)

    def group(k, g):
        return res.at[0, :, k, :, pl.ds(g * 64, 64), :]

    def half_group(k, g, r):
        return res.at[0, :, k, r, pl.ds(g * 64, 64), :]

    def slot(k, g, start=0, size=64):
        return res.at[1, :, k, 0, pl.ds(g * 64 + start, size), :]

    def step1(k):
        for q in range(2):
            res[0, q, k] = backward(2, q, k).astype(BF16).reshape(2, 256, 256)
        for d in range(2):
            send(half_group(k, 2, d), rxa0.at[d, :, k], rxa0_in[k][d], x_to[d])

    def step2(k, d):
        g = TO[d][1]
        arrived(rxa0.at[d, :, k], rxa0_in[k][d])
        add_into(half_group(k, g, d), rxa0.at[d, :, k])
        send(group(k, g), rxb0.at[d, :, k], rxb0_in[k], x_to[d])

    def step3(k):
        arrived(rxb0.at[:, :, k], rxb0_in[k])
        sy[:, k] = (
            res[0, :, k, 1, 0:64, :].astype(F32)
            + rxb0[0, :, k, 1].astype(F32)
            + rxb0[1, :, k, 1].astype(F32)
        ).astype(BF16)
        send(sy.at[:, k], ry0.at[:, k], ry0_in[k], y_to)

    home = [out_ref, gtok_ref]

    def go_home(a, k):
        dst = home[a].at[rows((p * 4 + z) * 64, 64), :]
        for dl in (1, 0):
            q = (l + dl) % 2
            if dl or k:
                send(fin.at[a, q, k], dst, home_in[a], dev(h, c, x, q, ring(z, k)))
            else:
                keep(fin.at[a, q, k], dst, home_in[a])

    def step4(k):
        arrived(ry0.at[:, k], ry0_in[k])
        fin[0, :, k] = (
            res[0, :, k, 0, 0:64, :].astype(F32)
            + rxb0[0, :, k, 0].astype(F32)
            + rxb0[1, :, k, 0].astype(F32)
            + ry0[:, k].astype(F32)
        ).astype(BF16)
        go_home(0, k)

    def slot1(k):
        arrived(ry1.at[:, k], ry1_in[k])
        add_into(res.at[1, :, k, 0], ry1.at[:, k])
        for d in range(2):
            send(slot(k, 2, 32 * d, 32), rxa1.at[d, :, k], rxa1_in[k][d], x_to[d])

    def slot2(k, d):
        g = TO[d][1]
        arrived(rxa1.at[d, :, k], rxa1_in[k][d])
        add_into(slot(k, g, 32 * d, 32), rxa1.at[d, :, k])
        send(slot(k, g), rxb1.at[d, :, k], rxb1_in[k], x_to[d])

    def slot3(k):
        arrived(rxb1.at[:, :, k], rxb1_in[k])
        fin[1, :, k] = (
            res[1, :, k, 0, 0:64, :].astype(F32)
            + rxb1[0, :, k].astype(F32)
            + rxb1[1, :, k].astype(F32)
        ).astype(BF16)
        go_home(1, k)

    sum_in = [take(4) for _ in range(3)]
    rza_in = [take(2) for _ in range(2)]
    rzb_in, gy_in = take(2), take(2)
    rza2_in, rzb2_in, gy2_in = take(2), take(), take(4)

    def grad0(w, k):
        for q in range(2):
            lhs = xin[w // 2, q, k].reshape(512, 256)
            wgo[w, q, k] = dot(lhs, act[w, 1 - c], TN).astype(BF16)
        send(wgo.at[w, :, k], wgi.at[w, :, k], sum_in[w][k], core_to)
        for q in range(2):
            lhs = xin[w // 2, q, k].reshape(512, 256)
            wgr[w, q, k] = dot(lhs, act[w, c], TN).astype(BF16)

    def both(w, k):
        arrived(wgi.at[w, :, k], sum_in[w][k])
        add_into(wgr.at[w, :, k], wgi.at[w, :, k])

    def grad1(w):
        both(w, 2)
        for d in range(2):
            send(wgr.at[w, :, 2, pl.ds(128 * d, 128), :], rza.at[w, d], rza_in[w][d], z_to[d])

    def grad2(w, d):
        k = TO[d][1]
        both(w, k)
        arrived(rza.at[w, d], rza_in[w][d])
        add_into(wgr.at[w, :, k, pl.ds(128 * d, 128), :], rza.at[w, d])
        send(wgr.at[w, :, k], rzb.at[w, d], rzb_in[w], z_to[d])

    def grad3(w):
        both(w, 0)
        arrived(rzb.at[w], rzb_in[w])
        gl[w] = (
            wgr[w, :, 0].astype(F32) + rzb[w, 0].astype(F32) + rzb[w, 1].astype(F32)
        ).astype(BF16)
        send(gl.at[w, 1 - l], gy.at[w], gy_in[w], l_to)

    def grad4(w):
        arrived(gy.at[w], gy_in[w])
        [ggate_ref, gup_ref][w][...] = gl[w, l].astype(F32) + gy[w].astype(F32)

    def down1(k):
        both(2, k)
        send(wgr.at[2, 1 - l, k], gy2.at[k], gy2_in[k], l_to)

    def down_sum(k):
        arrived(gy2.at[k], gy2_in[k])
        add_into(wgr.at[2, l, k], gy2.at[k])

    def down2():
        down_sum(2)
        for d in range(2):
            send(wgr.at[2, l, 2, pl.ds(128 * d, 128), :], rza2.at[d], rza2_in[d], z_to[d])

    def down3(d):
        k = TO[d][1]
        down_sum(k)
        arrived(rza2.at[d], rza2_in[d])
        add_into(wgr.at[2, l, k, pl.ds(128 * d, 128), :], rza2.at[d])
        send(wgr.at[2, l, k], rzb2.at[d], rzb2_in, z_to[d])

    def down4():
        down_sum(0)
        arrived(rzb2, rzb2_in)
        r = wgr[2, l, 0].astype(F32) + rzb2[0].astype(F32) + rzb2[1].astype(F32)
        gdown_ref[...] = r.T

    def finish():
        for a in (1, 0):
            arrived(home[a], home_in[a])

    for step, *args in (
        (scatter, 1, 0), (scatter, 0, 0), (scatter, 1, 1), (scatter, 1, 3), (scatter, 0, 1), (scatter, 0, 3),
        (w_own, 0), (w_own, 1), (scatter, 1, 2), (scatter, 0, 2), (d_first,), (cot_in, 0), (tok_in, 0),
        (cot_in, 3), (cot_in, 1), (tok_in, 3), (tok_in, 1), (x_second, 1, 0, 0, 0), (x_second, 1, 0, 0, 1),
        (x_second, 0, 0, 0, 0), (x_second, 0, 0, 0, 1), (tok_other, 0), (z_first, 0), (x_second, 1, 0, 3, 0),
        (x_second, 1, 0, 3, 1), (d_second, 0), (x_second, 1, 0, 1, 0), (x_second, 1, 0, 1, 1), (d_second, 1),
        (z_first, 1), (x_second, 0, 0, 3, 0), (x_second, 0, 0, 3, 1), (tok_other, 3), (weight_ready, 0, 0),
        (cot_in, 2), (tok_in, 2), (x_second, 0, 0, 1, 0), (x_second, 0, 0, 1, 1), (tok_other, 1), (x_last, 0),
        (weight_ready, 1, 0), (d_pass, 0), (x_second, 0, 1, 0, 0), (x_second, 0, 1, 0, 1), (z_second, 0, 0),
        (x_last, 3), (z_second, 0, 1), (x_last, 1), (d_last,), (d_pass, 3), (weight_ready, 2, 0),
        (x_second, 0, 1, 3, 0), (x_second, 0, 1, 3, 1), (weight_ready, 0, 3), (weight_ready, 0, 1),
        (x_second, 1, 0, 2, 0), (x_second, 1, 0, 2, 1), (d_pass, 1), (weight_ready, 2, 3),
        (x_second, 0, 0, 2, 0), (x_second, 0, 0, 2, 1), (z_second, 1, 0), (z_second, 1, 1), (d_pass, 2),
        (x_second, 0, 1, 1, 0), (x_second, 0, 1, 1, 1), (tok_other, 2), (weight_ready, 2, 1), (gathered, 0),
        (x_last, 2), (z_last, 0), (weight_ready, 1, 3), (gathered, 3), (weight_ready, 1, 1),
        (weight_ready, 2, 2), (gathered, 1), (products, 0), (x_second, 0, 1, 2, 0), (x_second, 0, 1, 2, 1),
        (z_last, 1), (weight_ready, 0, 2), (products, 1), (products, 2), (gathered, 2), (weight_ready, 1, 2),
        (activate, 0), (activate, 1), (slot0, 2), (step1, 2), (grad0, 0, 2), (slot0, 1), (step1, 1),
        (slot0, 3), (step1, 3), (grad0, 1, 2), (grad1, 0), (step2, 2, 0), (step2, 2, 1), (grad0, 2, 2),
        (grad0, 0, 1), (grad0, 0, 3), (step2, 1, 0), (step2, 1, 1), (grad0, 1, 1), (grad0, 2, 1), (grad1, 1),
        (step2, 3, 0), (step2, 3, 1), (grad0, 1, 3), (slot1, 2), (down1, 2), (slot0, 0), (grad2, 0, 0),
        (grad2, 0, 1), (step1, 0), (step3, 2), (down1, 1), (grad0, 2, 3), (grad0, 0, 0), (grad0, 1, 0),
        (grad0, 2, 0), (grad2, 1, 0), (step3, 1), (grad2, 1, 1), (slot1, 1), (down2,), (down1, 3), (step3, 3),
        (down1, 0), (slot2, 2, 0), (slot2, 2, 1), (step2, 0, 0), (step2, 0, 1), (grad3, 0), (slot2, 1, 0),
        (slot2, 1, 1), (slot1, 3), (slot3, 2), (step3, 0), (grad3, 1), (slot1, 0), (slot3, 1), (down3, 0),
        (down3, 1), (slot2, 3, 0), (slot2, 3, 1), (grad4, 0), (step4, 2), (step4, 1), (slot2, 0, 0),
        (slot2, 0, 1), (step4, 3), (grad4, 1), (slot3, 3), (step4, 0), (down4,), (slot3, 0), (finish,),
    ):
        step(*args)
    for copy in pool:
        if copy is not None:
            copy.wait_send()


def place(*refs):
    held, sems = refs[10:15], refs[15]
    come = [pltpu.make_async_copy(refs[n], held[n], sems.at[n]) for n in range(5)]
    go = [pltpu.make_async_copy(held[n], refs[5 + n], sems.at[5 + n]) for n in range(5)]
    for copy in come:
        copy.start()
    for first, then in zip(come, go):
        first.wait()
        then.start()
    for copy in go:
        copy.wait()


def on_device(tokens, gate_weight, up_weight, down_weight, cotangent):
    vmem = pl.BlockSpec(memory_space=pltpu.VMEM)
    anywhere = pl.BlockSpec(memory_space=pl.ANY)
    shapes = [jax.ShapeDtypeStruct((512, 256), BF16)] * 2
    shapes += [jax.ShapeDtypeStruct((256, 256), F32)] * 3
    results = pl.pallas_call(
        kernel,
        name="swiglu",
        out_shape=shapes,
        in_specs=[anywhere] * 5,
        out_specs=[anywhere] * 2 + [vmem] * 3,
        scratch_shapes=[
            pltpu.VMEM((256, 256), BF16),
            pltpu.VMEM((2, 2, 4, 2, 256, 256), BF16),
            pltpu.VMEM((3, 2, 2, 4, 256, 256), BF16),
            pltpu.VMEM((3, 2, 512, 256), F32),
            pltpu.VMEM((3, 2, 512, 256), BF16),
            pltpu.VMEM((2, 2, 4, 2, 256, 256), BF16),
            pltpu.VMEM((3, 2, 4, 256, 256), BF16),
            pltpu.VMEM((3, 2, 4, 256, 256), BF16),
            pltpu.VMEM((3, 2, 4, 256, 256), BF16),
            pltpu.VMEM((2, 2, 4, 64, 256), BF16),
            pltpu.VMEM((2, 2, 4, 32, 256), BF16),
            pltpu.VMEM((2, 2, 4, 2, 64, 256), BF16),
            pltpu.VMEM((2, 2, 4, 64, 256), BF16),
            pltpu.VMEM((2, 4, 64, 256), BF16),
            pltpu.VMEM((2, 4, 256, 256), BF16),
            pltpu.VMEM((2, 4, 64, 256), BF16),
            pltpu.VMEM((2, 2, 4, 64, 256), BF16),
            pltpu.VMEM((2, 2, 2, 128, 256), BF16),
            pltpu.VMEM((2, 2, 2, 256, 256), BF16),
            pltpu.VMEM((2, 256, 256), BF16),
            pltpu.VMEM((2, 2, 256, 256), BF16),
            pltpu.VMEM((2, 128, 256), BF16),
            pltpu.VMEM((2, 256, 256), BF16),
            pltpu.VMEM((4, 256, 256), BF16),
            pltpu.SemaphoreType.DMA((N_SEND,)),
            pltpu.SemaphoreType.DMA((N_RECV,)),
            pltpu.SemaphoreType.DMA,
        ],
        compiler_params=pltpu.CompilerParams(
            collective_id=0, has_side_effects=True, vmem_limit_bytes=60 << 20
        ),
        cost_estimate=pl.CostEstimate(
            flops=9 * 2 * 1024 * 1024 * 512, bytes_accessed=3 << 20, transcendentals=1024 * 256
        ),
    )(
        tokens.reshape(512, 256),
        gate_weight,
        up_weight,
        down_weight,
        cotangent.reshape(512, 256),
    )
    output, grad_tokens, grad_gate, grad_up, grad_down = pl.pallas_call(
        place,
        name="place",
        out_shape=shapes,
        in_specs=[anywhere] * 5,
        out_specs=[anywhere] * 5,
        scratch_shapes=[pltpu.VMEM(s.shape, s.dtype) for s in shapes]
        + [pltpu.SemaphoreType.DMA((10,))],
    )(*results)
    return (
        output.reshape(2, 256, 256),
        grad_tokens.reshape(2, 256, 256),
        grad_gate,
        grad_up,
        grad_down,
    )


def solution(mesh):
    in_specs = (
        P(None, ("inp", "wt"), "out"),
        P("out", ("wt", "inp")),
        P("out", ("wt", "inp")),
        P(("wt", "inp"), "out"),
        P(None, ("inp", "wt"), "out"),
    )
    out_specs = (
        P(None, ("inp", "wt"), "out"),
        P(None, ("inp", "wt"), "out"),
        P("out", ("wt", "inp")),
        P("out", ("wt", "inp")),
        P(("wt", "inp"), "out"),
    )
    return jax.shard_map(
        on_device, mesh=mesh, in_specs=in_specs, out_specs=out_specs, check_vma=False
    )
```

time: 538 us -> 84.2 us (0.16)
  waiting for transfers between devices: 451 us -> 0 us
  Pallas kernels: 0 us -> 82.5 us
  matrix products: 35.9 us -> 0 us
  blocking collectives: 26.7 us -> 0 us
  between operations: 14 us -> 0.8 us
    reduce_scatter x8 -> x0, waiting for transfers between devices: 282 us -> none  [the longest x1 54.2 us: on_device(): lax.psum_scatter(gate_part.astype(jnp.bfloat16), 'out', scatter_dimension...]
    all_gather x5 -> x0, waiting for transfers between devices: 166 us -> none  [the longest x1 50.1 us: on_device(): lax.all_gather(gate_act_own, 'out', axis=1, tiled=True)]
    pallas_call x0 -> x2, Pallas kernels: none -> 82.5 us  [the longest x1 80.4 us: on_device(): pl.pallas_call(kernel, name='swiglu', out_shape=shapes, in_specs=[anywher...]
    dot_general x9 -> x0, matrix products: 35.9 us -> none  [the longest x1 4.57 us: on_device(): jnp.einsum('btd,df->btf', in_block, up_full, preferred_element_type=jnp.f...]
    all_gather x3 -> x0, blocking collectives: 26.7 us -> none  [the longest x1 9.17 us: on_device(): lax.all_gather(up_weight, 'inp', axis=1, tiled=True)]
  transfers between devices with their start and end apart: 13 -> 0, of which waited for: 12 -> 0; matrix products, arithmetic and copies ran while one was open for 8% -> 0% of each run, Pallas kernels for 0% -> 0%
where the time goes in v3:
time: 84.2 us; the launch traced here: 83.3 us
  Pallas kernels  82.5 us (98%)
    pallas_call x1, Pallas kernels, on_device(): pl.pallas_call(kernel, name='swiglu', out_shape=shapes, in_specs=[anywher...  80.4 us
    pallas_call x1, Pallas kernels, on_device(): pl.pallas_call(place, name='place', out_shape=shapes, in_specs=[anywhere]...  2.09 us

profile of v3, /device:TPU:0, one launch (start us, length us, event | category | flops | bytes accessed | tf_op | source)
XLA Modules:
  0.0 83.3 jit_solution(12399017388729987040)
XLA Ops:
  0.6 80.4 %swiglu.1 = (bf16[512,256]{1,0:T(8,128)(2,1)}, bf16[512,256]{1,0:T(8,128)(2,1)}, f32[256,256]{1,0:T(8,128)}, f32[256,256]{1,0:T(8,128)}, f32[256,256]{1,0:T(8,128)}) custom-call(bf16[512,256]{1,0:T(8,128)(2,1)} %bitcast.4, bf16[256,256]{1,0:T(8,128)(2,1)} %gate_w.1, bf16[256,256]{1,0:T(8,128)(2,1)} %up_w.1, bf16[256,256]{1,0:T(8,128)(2,1)} %down_w.1, ...), custom_call_target="tpu_custom_call" | custom-call | flops 9663676416 | bytes 3145728 | tf_op jit(solution)/shard_map/swiglu/pallas_call | solution.py:446
  81.0 2.1 %place.1 = (bf16[512,256]{1,0:T(8,128)(2,1)}, bf16[512,256]{1,0:T(8,128)(2,1)}, f32[256,256]{1,0:T(8,128)}, f32[256,256]{1,0:T(8,128)}, f32[256,256]{1,0:T(8,128)}) custom-call(bf16[512,256]{1,0:T(8,128)(2,1)} %get-tuple-element.15.refs_0_, bf16[512,256]{1,0:T(8,128)(2,1)} %get-tuple-element.16.refs_1_, f32[256,256]{1,0:T(8,128)} %get-tuple-element.17.refs_2_, ...), custom_call_target="tpu_custom_call" | custom-call | tf_op jit(solution)/shard_map/place/pallas_call | solution.py:494

commit v4 on v3

--- a/solution.py
+++ b/solution.py
@@ -30,10 +30,16 @@
 
 
 N_SEND = 80
-N_RECV = 150
+N_RECV = 190
 GATHER = (0, 1, 3, 2)
+CROSS_IN = (0,)
+CROSS_OUT = (2,)
 FROM = ((0, 3), (1, 1))
 TO = ((0, 1), (1, 3))
+
+
+def ways_in(k):
+    return ((0, 0), (0, 1), (1, 0), (1, 1)) if k in CROSS_IN else ((0, 0), (0, 1), (1, 0))
 
 
 def kernel(
@@ -99,8 +105,8 @@
 
     source = [tok, cot]
     a2a_in = [take(4), take(4)]
-    x_hop = {(a, r, k): [take(2), take()] for k in range(4) for a, r in ((1, 0), (0, 0), (0, 1))}
-    y0_in, y1_in = take(4), take(4)
+    x_hop = {(a, r, k): [take(2), take()] for k in range(4) for a, r in ways_in(k)}
+    y0_in, y1_in = [take(4), [take() if k in CROSS_IN else None for k in range(4)]], take(4)
     w_in = [take(1), take(1), take(4)]
     z_hop = [[take(2), take()] for _ in range(3)]
     pass_in = [take(4) for _ in range(3)]
@@ -119,33 +125,54 @@
             else:
                 keep(src, dst, a2a_in[a][k])
 
+    def y_first(a, k):
+        return a == 0 or k in CROSS_IN
+
+    def early(a):
+        src = source[a].at[rows((p * 4 + z) * 64, 64), :]
+        for d, g in FROM:
+            dst = xin.at[a, l, 0, 0, pl.ds(g * 64, 64), :]
+            send(src, dst, x_hop[a, 0, 0][0][d], x_to[d])
+        sem = y0_in[a][0] if y_first(a, 0) else y1_in[0]
+        send(src, xin.at[a, l, 0, 1, pl.ds(0, 64), :], sem, y_to)
+
     def x_first(a, r, k):
         for d, g in FROM:
-            send(x_slot(a, k, 0, r), x_slot(a, k, g, r), x_hop[a, r, k][0][d], x_to[d])
+            src, dst = x_slot(a, k, 0, r), x_slot(a, k, g, r)
+            if r == 0 and k == 0:
+                src = xin.at[a, 1 - l, 0, 0, pl.ds(0, 64), :]
+                dst = xin.at[a, 1 - l, 0, 0, pl.ds(g * 64, 64), :]
+            send(src, dst, x_hop[a, r, k][0][d], x_to[d])
+
+    def y_own(a, k, sem):
+        src, dst = x_slot(a, k, 0), x_slot(a, k, 0, 1)
+        if k == 0:
+            src = xin.at[a, 1 - l, 0, 0, pl.ds(0, 64), :]
+            dst = xin.at[a, 1 - l, 0, 1, pl.ds(0, 64), :]
+        send(src, dst, sem, y_to)
 
     def y1_send(k, g):
         send(x_slot(1, k, g), x_slot(1, k, g, 1), y1_in[k], y_to)
 
-    def cot_in(k):
-        arrived(x_slot(1, k, 0), a2a_in[1][k])
-        x_first(1, 0, k)
-        y1_send(k, 0)
-
-    def tok_in(k):
-        arrived(x_slot(0, k, 0), a2a_in[0][k])
-        send(x_slot(0, k, 0), x_slot(0, k, 0, 1), y0_in[k], y_to)
-        x_first(0, 0, k)
-
-    def tok_other(k):
-        arrived(x_slot(0, k, 0, 1), y0_in[k])
-        x_first(0, 1, k)
+    def x_in(a, k):
+        arrived(x_slot(a, k, 0), a2a_in[a][k])
+        if y_first(a, k):
+            y_own(a, k, y0_in[a][k])
+            x_first(a, 0, k)
+        else:
+            x_first(a, 0, k)
+            y_own(a, k, y1_in[k])
+
+    def x_other(a, k):
+        arrived(x_slot(a, k, 0, 1), y0_in[a][k])
+        x_first(a, 1, k)
 
     def x_second(a, r, k, d):
         g = FROM[d][1]
         arrived(x_slot(a, k, g, r), x_hop[a, r, k][0][d])
         half = (32 * d, 32)
         send(x_slot(a, k, g, r, *half), x_slot(a, k, 2, r, *half), x_hop[a, r, k][1], x_to[d])
-        if a == 1:
+        if not y_first(a, k):
             y1_send(k, g)
 
     def x_last(k):
@@ -153,9 +180,12 @@
         y1_send(k, 2)
 
     def gathered(k):
-        for r in range(2):
-            arrived(x_slot(0, k, 2, r), x_hop[0, r, k][1])
-        arrived(xin.at[1, :, k, 1], y1_in[k])
+        for a in range(2):
+            if y_first(a, k):
+                for r in range(2):
+                    arrived(x_slot(a, k, 2, r), x_hop[a, r, k][1])
+            else:
+                arrived(xin.at[a, :, k, 1], y1_in[k])
 
     def w_blocks(w, k, start=0, size=256):
         return wts.at[w, c, :, k, pl.ds(start, size), :]
@@ -211,8 +241,8 @@
     def weight_ready(w, k):
         arrived(wts.at[w, 1 - c, :, k], pass_in[w][k])
 
-    early = [(q, k) for q in range(2) for k in GATHER[:3]]
-    late = [(q, GATHER[3]) for q in range(2)]
+    first_blocks = [(q, k) for q in range(2) for k in GATHER[:3]]
+    last_blocks = [(q, GATHER[3]) for q in range(2)]
 
     def product(w, f, blocks):
         lhs = jnp.concatenate([xin[w // 2, q, k].reshape(512, 256) for q, k in blocks], axis=1)
@@ -221,61 +251,61 @@
 
     def products(w):
         for f in range(2):
-            part[w, f] = product(w, f, early)
+            part[w, f] = product(w, f, first_blocks)
 
     def activate(f):
-        gate = part[0, f] + product(0, f, late)
-        up = part[1, f] + product(1, f, late)
-        back = part[2, f] + product(2, f, late)
+        gate = part[0, f] + product(0, f, last_blocks)
+        up = part[1, f] + product(1, f, last_blocks)
+        back = part[2, f] + product(2, f, last_blocks)
         s = jax.nn.sigmoid(gate)
         silu = gate * s
         act[0, f] = (back * up * (s * (1.0 + gate * (1.0 - s)))).astype(BF16)
         act[1, f] = (back * silu).astype(BF16)
         act[2, f] = (silu * up).astype(BF16)
 
-    ry0_in, ry1_in, rxb0_in, rxb1_in = (take(4) for _ in range(4))
-    rxa0_in, rxa1_in = ([take(2) for _ in range(4)] for _ in range(2))
+    ry1_in, rxb1_in = take(4), take(4)
+    rxa1_in = [take(2) for _ in range(4)]
+    last = [(0, k) for k in range(4)] + [(1, k) for k in CROSS_OUT]
+    rxa0_in, rxb0_in, ry0_in = {q: take(2) for q in last}, {q: take() for q in last}, {q: take() for q in last}
     home_in = take(2)
 
     def backward(w, q, k):
         lhs = jnp.concatenate([act[w, 0], act[w, 1]], axis=1)
         return dot(lhs, jnp.concatenate([wts[w, 0, q, k], wts[w, 1, q, k]], axis=1), NT)
 
-    def slot0(k):
+    def output(a, k):
         for q in range(2):
-            r = backward(0, q, k) + backward(1, q, k)
-            res[1, q, k] = r.astype(BF16).reshape(2, 256, 256)
-        send(res.at[1, :, k, 1], ry1.at[:, k], ry1_in[k], y_to)
-
-    def group(k, g):
-        return res.at[0, :, k, :, pl.ds(g * 64, 64), :]
-
-    def half_group(k, g, r):
-        return res.at[0, :, k, r, pl.ds(g * 64, 64), :]
+            r = backward(0, q, k) + backward(1, q, k) if a else backward(2, q, k)
+            res[a, q, k] = r.astype(BF16).reshape(2, 256, 256)
+
+    def group(a, k, g):
+        return res.at[a, :, k, :, pl.ds(g * 64, 64), :]
+
+    def half_group(a, k, g, r):
+        return res.at[a, :, k, r, pl.ds(g * 64, 64), :]
 
     def slot(k, g, start=0, size=64):
         return res.at[1, :, k, 0, pl.ds(g * 64 + start, size), :]
 
-    def step1(k):
-        for q in range(2):
-            res[0, q, k] = backward(2, q, k).astype(BF16).reshape(2, 256, 256)
+    def step1(a, k):
+        output(a, k)
         for d in range(2):
-            send(half_group(k, 2, d), rxa0.at[d, :, k], rxa0_in[k][d], x_to[d])
-
-    def step2(k, d):
+            send(half_group(a, k, 2, d), rxa0.at[a, d, :, k], rxa0_in[a, k][d], x_to[d])
+
+    def step2(a, k, d):
         g = TO[d][1]
-        arrived(rxa0.at[d, :, k], rxa0_in[k][d])
-        add_into(half_group(k, g, d), rxa0.at[d, :, k])
-        send(group(k, g), rxb0.at[d, :, k], rxb0_in[k], x_to[d])
-
-    def step3(k):
-        arrived(rxb0.at[:, :, k], rxb0_in[k])
-        sy[:, k] = (
-            res[0, :, k, 1, 0:64, :].astype(F32)
-            + rxb0[0, :, k, 1].astype(F32)
-            + rxb0[1, :, k, 1].astype(F32)
+        arrived(rxa0.at[a, d, :, k], rxa0_in[a, k][d])
+        add_into(half_group(a, k, g, d), rxa0.at[a, d, :, k])
+        send(group(a, k, g), rxb0.at[a, d, :, k], rxb0_in[a, k], x_to[d])
+
+    def step3(a, k):
+        arrived(rxb0.at[a, :, :, k], rxb0_in[a, k])
+        sy[a, :, k] = (
+            res[a, :, k, 1, 0:64, :].astype(F32)
+            + rxb0[a, 0, :, k, 1].astype(F32)
+            + rxb0[a, 1, :, k, 1].astype(F32)
         ).astype(BF16)
-        send(sy.at[:, k], ry0.at[:, k], ry0_in[k], y_to)
+        send(sy.at[a, :, k], ry0.at[a, :, k], ry0_in[a, k], y_to)
 
     home = [out_ref, gtok_ref]
 
@@ -288,15 +318,19 @@
             else:
                 keep(fin.at[a, q, k], dst, home_in[a])
 
-    def step4(k):
-        arrived(ry0.at[:, k], ry0_in[k])
-        fin[0, :, k] = (
-            res[0, :, k, 0, 0:64, :].astype(F32)
-            + rxb0[0, :, k, 0].astype(F32)
-            + rxb0[1, :, k, 0].astype(F32)
-            + ry0[:, k].astype(F32)
+    def step4(a, k):
+        arrived(ry0.at[a, :, k], ry0_in[a, k])
+        fin[a, :, k] = (
+            res[a, :, k, 0, 0:64, :].astype(F32)
+            + rxb0[a, 0, :, k, 0].astype(F32)
+            + rxb0[a, 1, :, k, 0].astype(F32)
+            + ry0[a, :, k].astype(F32)
         ).astype(BF16)
-        go_home(0, k)
+        go_home(a, k)
+
+    def slot0(k):
+        output(1, k)
+        send(res.at[1, :, k, 1], ry1.at[:, k], ry1_in[k], y_to)
 
     def slot1(k):
         arrived(ry1.at[:, k], ry1_in[k])
@@ -392,32 +426,35 @@
             arrived(home[a], home_in[a])
 
     for step, *args in (
-        (scatter, 1, 0), (scatter, 0, 0), (scatter, 1, 1), (scatter, 1, 3), (scatter, 0, 1), (scatter, 0, 3),
-        (w_own, 0), (w_own, 1), (scatter, 1, 2), (scatter, 0, 2), (d_first,), (cot_in, 0), (tok_in, 0),
-        (cot_in, 3), (cot_in, 1), (tok_in, 3), (tok_in, 1), (x_second, 1, 0, 0, 0), (x_second, 1, 0, 0, 1),
-        (x_second, 0, 0, 0, 0), (x_second, 0, 0, 0, 1), (tok_other, 0), (z_first, 0), (x_second, 1, 0, 3, 0),
-        (x_second, 1, 0, 3, 1), (d_second, 0), (x_second, 1, 0, 1, 0), (x_second, 1, 0, 1, 1), (d_second, 1),
-        (z_first, 1), (x_second, 0, 0, 3, 0), (x_second, 0, 0, 3, 1), (tok_other, 3), (weight_ready, 0, 0),
-        (cot_in, 2), (tok_in, 2), (x_second, 0, 0, 1, 0), (x_second, 0, 0, 1, 1), (tok_other, 1), (x_last, 0),
-        (weight_ready, 1, 0), (d_pass, 0), (x_second, 0, 1, 0, 0), (x_second, 0, 1, 0, 1), (z_second, 0, 0),
-        (x_last, 3), (z_second, 0, 1), (x_last, 1), (d_last,), (d_pass, 3), (weight_ready, 2, 0),
-        (x_second, 0, 1, 3, 0), (x_second, 0, 1, 3, 1), (weight_ready, 0, 3), (weight_ready, 0, 1),
-        (x_second, 1, 0, 2, 0), (x_second, 1, 0, 2, 1), (d_pass, 1), (weight_ready, 2, 3),
-        (x_second, 0, 0, 2, 0), (x_second, 0, 0, 2, 1), (z_second, 1, 0), (z_second, 1, 1), (d_pass, 2),
-        (x_second, 0, 1, 1, 0), (x_second, 0, 1, 1, 1), (tok_other, 2), (weight_ready, 2, 1), (gathered, 0),
-        (x_last, 2), (z_last, 0), (weight_ready, 1, 3), (gathered, 3), (weight_ready, 1, 1),
-        (weight_ready, 2, 2), (gathered, 1), (products, 0), (x_second, 0, 1, 2, 0), (x_second, 0, 1, 2, 1),
-        (z_last, 1), (weight_ready, 0, 2), (products, 1), (products, 2), (gathered, 2), (weight_ready, 1, 2),
-        (activate, 0), (activate, 1), (slot0, 2), (step1, 2), (grad0, 0, 2), (slot0, 1), (step1, 1),
-        (slot0, 3), (step1, 3), (grad0, 1, 2), (grad1, 0), (step2, 2, 0), (step2, 2, 1), (grad0, 2, 2),
-        (grad0, 0, 1), (grad0, 0, 3), (step2, 1, 0), (step2, 1, 1), (grad0, 1, 1), (grad0, 2, 1), (grad1, 1),
-        (step2, 3, 0), (step2, 3, 1), (grad0, 1, 3), (slot1, 2), (down1, 2), (slot0, 0), (grad2, 0, 0),
-        (grad2, 0, 1), (step1, 0), (step3, 2), (down1, 1), (grad0, 2, 3), (grad0, 0, 0), (grad0, 1, 0),
-        (grad0, 2, 0), (grad2, 1, 0), (step3, 1), (grad2, 1, 1), (slot1, 1), (down2,), (down1, 3), (step3, 3),
-        (down1, 0), (slot2, 2, 0), (slot2, 2, 1), (step2, 0, 0), (step2, 0, 1), (grad3, 0), (slot2, 1, 0),
-        (slot2, 1, 1), (slot1, 3), (slot3, 2), (step3, 0), (grad3, 1), (slot1, 0), (slot3, 1), (down3, 0),
-        (down3, 1), (slot2, 3, 0), (slot2, 3, 1), (grad4, 0), (step4, 2), (step4, 1), (slot2, 0, 0),
-        (slot2, 0, 1), (step4, 3), (grad4, 1), (slot3, 3), (step4, 0), (down4,), (slot3, 0), (finish,),
+        (scatter, 1, 0), (scatter, 1, 1), (scatter, 1, 3), (early, 0), (scatter, 1, 2), (scatter, 0, 0),
+        (w_own, 0), (early, 1), (scatter, 0, 1), (scatter, 0, 3), (scatter, 0, 2), (w_own, 1), (d_first,),
+        (x_in, 1, 0), (x_in, 1, 3), (x_in, 1, 1), (x_in, 1, 2), (x_in, 0, 0), (x_other, 1, 0),
+        (x_second, 1, 0, 0, 0), (x_second, 1, 0, 0, 1), (x_second, 1, 0, 3, 0), (x_second, 1, 0, 3, 1),
+        (z_first, 0), (x_second, 1, 0, 1, 0), (x_second, 1, 0, 1, 1), (x_in, 0, 3), (x_in, 0, 1),
+        (x_second, 1, 0, 2, 0), (x_second, 1, 0, 2, 1), (d_second, 0), (d_second, 1), (x_second, 0, 0, 0, 0),
+        (x_second, 0, 0, 0, 1), (weight_ready, 0, 0), (x_in, 0, 2), (x_other, 0, 0), (x_second, 1, 1, 0, 0),
+        (x_second, 1, 1, 0, 1), (z_first, 1), (x_last, 3), (x_last, 1), (weight_ready, 1, 0),
+        (x_second, 0, 0, 3, 0), (x_second, 0, 0, 3, 1), (d_pass, 0), (z_second, 0, 0), (z_second, 0, 1),
+        (x_second, 0, 0, 1, 0), (x_second, 0, 0, 1, 1), (d_last,), (x_last, 2), (x_other, 0, 3),
+        (weight_ready, 2, 0), (d_pass, 3), (weight_ready, 0, 3), (x_other, 0, 1), (weight_ready, 0, 1),
+        (x_second, 0, 0, 2, 0), (x_second, 0, 0, 2, 1), (weight_ready, 2, 3), (x_second, 0, 1, 0, 0),
+        (x_second, 0, 1, 0, 1), (d_pass, 1), (z_second, 1, 0), (z_second, 1, 1), (x_other, 0, 2),
+        (weight_ready, 2, 1), (d_pass, 2), (x_second, 0, 1, 3, 0), (x_second, 0, 1, 3, 1),
+        (weight_ready, 1, 3), (x_second, 0, 1, 1, 0), (x_second, 0, 1, 1, 1), (weight_ready, 1, 1),
+        (z_last, 0), (weight_ready, 2, 2), (gathered, 0), (weight_ready, 0, 2), (x_second, 0, 1, 2, 0),
+        (x_second, 0, 1, 2, 1), (z_last, 1), (gathered, 3), (gathered, 1), (products, 0), (products, 1),
+        (weight_ready, 1, 2), (products, 2), (gathered, 2), (activate, 0), (activate, 1), (step1, 0, 2),
+        (step1, 1, 2), (slot0, 1), (grad0, 0, 2), (slot0, 3), (step1, 0, 1), (step1, 0, 3), (grad0, 1, 2),
+        (step2, 0, 2, 0), (grad1, 0), (step2, 0, 2, 1), (slot0, 0), (step2, 1, 2, 0), (step2, 1, 2, 1),
+        (grad0, 2, 2), (step1, 0, 0), (grad1, 1), (grad0, 0, 1), (step2, 0, 1, 0), (step2, 0, 1, 1),
+        (grad0, 0, 3), (grad0, 1, 1), (down1, 2), (step2, 0, 3, 0), (step2, 0, 3, 1), (grad0, 2, 1),
+        (grad0, 1, 3), (grad0, 2, 3), (grad2, 0, 0), (grad2, 0, 1), (slot1, 1), (grad0, 0, 0), (grad0, 1, 0),
+        (step3, 0, 2), (down1, 1), (grad0, 2, 0), (grad2, 1, 0), (down1, 3), (grad2, 1, 1), (down2,),
+        (step3, 1, 2), (down1, 0), (slot1, 3), (step2, 0, 0, 0), (step2, 0, 0, 1), (step3, 0, 1), (grad3, 0),
+        (slot1, 0), (step3, 0, 3), (slot2, 1, 0), (slot2, 1, 1), (step4, 0, 2), (slot2, 3, 0), (slot2, 3, 1),
+        (step4, 1, 2), (grad3, 1), (down3, 0), (step4, 0, 1), (step3, 0, 0), (grad4, 0), (down3, 1),
+        (slot2, 0, 0), (slot2, 0, 1), (step4, 0, 3), (slot3, 1), (slot3, 3), (step4, 0, 0), (grad4, 1),
+        (slot3, 0), (down4,), (finish,),
     ):
         step(*args)
     for copy in pool:
@@ -459,13 +496,13 @@
             pltpu.VMEM((3, 2, 4, 256, 256), BF16),
             pltpu.VMEM((3, 2, 4, 256, 256), BF16),
             pltpu.VMEM((3, 2, 4, 256, 256), BF16),
+            pltpu.VMEM((2, 2, 2, 4, 64, 256), BF16),
+            pltpu.VMEM((2, 2, 4, 32, 256), BF16),
+            pltpu.VMEM((2, 2, 2, 4, 2, 64, 256), BF16),
             pltpu.VMEM((2, 2, 4, 64, 256), BF16),
-            pltpu.VMEM((2, 2, 4, 32, 256), BF16),
-            pltpu.VMEM((2, 2, 4, 2, 64, 256), BF16),
             pltpu.VMEM((2, 2, 4, 64, 256), BF16),
-            pltpu.VMEM((2, 4, 64, 256), BF16),
             pltpu.VMEM((2, 4, 256, 256), BF16),
-            pltpu.VMEM((2, 4, 64, 256), BF16),
+            pltpu.VMEM((2, 2, 4, 64, 256), BF16),
             pltpu.VMEM((2, 2, 4, 64, 256), BF16),
             pltpu.VMEM((2, 2, 2, 128, 256), BF16),
             pltpu.VMEM((2, 2, 2, 256, 256), BF16),

time: 84.2 us -> 83.3 us (0.989)
  no operation moved by 1% of the time
where the time goes in v4:
time: 83.3 us; the launch traced here: 83.2 us
  Pallas kernels  82.4 us (99%)
    pallas_call x1, Pallas kernels, on_device(): pl.pallas_call(kernel, name='swiglu', out_shape=shapes, in_specs=[anywher...  80.3 us
    pallas_call x1, Pallas kernels, on_device(): pl.pallas_call(place, name='place', out_shape=shapes, in_specs=[anywhere]...  2.09 us

profile of v4, /device:TPU:0, one launch (start us, length us, event | category | flops | bytes accessed | tf_op | source)
XLA Modules:
  0.0 83.2 jit_solution(12936470027209851004)
XLA Ops:
  0.6 80.3 %swiglu.1 = (bf16[512,256]{1,0:T(8,128)(2,1)}, bf16[512,256]{1,0:T(8,128)(2,1)}, f32[256,256]{1,0:T(8,128)}, f32[256,256]{1,0:T(8,128)}, f32[256,256]{1,0:T(8,128)}) custom-call(bf16[512,256]{1,0:T(8,128)(2,1)} %bitcast.4, bf16[256,256]{1,0:T(8,128)(2,1)} %gate_w.1, bf16[256,256]{1,0:T(8,128)(2,1)} %up_w.1, bf16[256,256]{1,0:T(8,128)(2,1)} %down_w.1, ...), custom_call_target="tpu_custom_call" | custom-call | flops 9663676416 | bytes 3145728 | tf_op jit(solution)/shard_map/swiglu/pallas_call | solution.py:483
  80.9 2.1 %place.1 = (bf16[512,256]{1,0:T(8,128)(2,1)}, bf16[512,256]{1,0:T(8,128)(2,1)}, f32[256,256]{1,0:T(8,128)}, f32[256,256]{1,0:T(8,128)}, f32[256,256]{1,0:T(8,128)}) custom-call(bf16[512,256]{1,0:T(8,128)(2,1)} %get-tuple-element.15.refs_0_, bf16[512,256]{1,0:T(8,128)(2,1)} %get-tuple-element.16.refs_1_, f32[256,256]{1,0:T(8,128)} %get-tuple-element.17.refs_2_, ...), custom_call_target="tpu_custom_call" | custom-call | tf_op jit(solution)/shard_map/place/pallas_call | solution.py:531
